TPU v7x, 32 devices: a whole 2x2x4 slice. The times are simulated.
32 devices in a mesh: blk: 16 (over z, y, core), grp: 2 (over x).
Axes of the slice: x: 2, y: 2, z: 4, core: 2. Of those that a mesh axis runs over, the one named last changes fastest.
Arguments:
- queries: bfloat16 [8192, 2048], P(('blk', 'grp')), may hold values from -100 to 100
- keys: bfloat16 [8192, 1024], P(('blk', 'grp')), may hold values from -4 to 4
- values: bfloat16 [8192, 1024], P(('blk', 'grp')), may hold values from -6 to 6
Outputs:
- attended: bfloat16 [8192, 2048], P(('blk', 'grp'))
All inputs are finite; a program needn't handle non-finite values.
Results may differ from a plain program's by a relative error of at most 0.0049.
Values may be sent and summed in bfloat16 or wider, within the bound.
A program may use at most 64 MiB of HBM per device.

v0:
```python
import jax
import jax.numpy as jnp
from jax import lax
from jax.sharding import PartitionSpec as P

HEADS = 16
KV_HEADS = 8
HEAD_DIM = 128
WINDOW = 1024


def from_behind(x, axis, by):
    peers = lax.axis_size(axis)
    pairs = [(i, i + by) for i in range(peers) if 0 <= i + by < peers]
    return lax.ppermute(x, axis, pairs)


def attend_block(query_rows, key_win, value_win, block_index):
    tok_rows = query_rows.shape[0]
    group_size = HEADS // KV_HEADS
    span_rows = key_win.shape[0]
    row_ids = jnp.arange(tok_rows, dtype=jnp.int32)[:, None]
    col_ids = jnp.arange(span_rows, dtype=jnp.int32)[None, :]
    position = block_index * tok_rows - WINDOW + col_ids
    allowed = (col_ids > row_ids) & (col_ids <= row_ids + WINDOW) & (position >= 0)

    def head_group(head_index):
        query_part = lax.dynamic_slice_in_dim(
            query_rows, head_index * group_size * HEAD_DIM, group_size * HEAD_DIM, 1
        )
        query_part = query_part.reshape(tok_rows, group_size, HEAD_DIM)
        key_part = lax.dynamic_slice_in_dim(key_win, head_index * HEAD_DIM, HEAD_DIM, 1)
        value_part = lax.dynamic_slice_in_dim(value_win, head_index * HEAD_DIM, HEAD_DIM, 1)
        score = jnp.einsum(
            "thd,kd->htk", query_part, key_part, preferred_element_type=jnp.float32
        ) * HEAD_DIM ** (-0.5)
        score = jnp.where(allowed[None], score, jnp.float32(-1e30))
        largest = jnp.max(score, axis=2, keepdims=True)
        expo = jnp.where(allowed[None], jnp.exp(score - largest), jnp.float32(0.0))
        total = jnp.sum(expo, axis=2, keepdims=True)
        weight = (expo / total).astype(jnp.bfloat16)
        output = jnp.einsum("htk,kd->thd", weight, value_part, preferred_element_type=jnp.float32)
        return output.astype(jnp.bfloat16).reshape(tok_rows, group_size * HEAD_DIM)

    parts = lax.map(head_group, jnp.arange(KV_HEADS, dtype=jnp.int32))
    return jnp.transpose(parts, (1, 0, 2)).reshape(tok_rows, HEADS * HEAD_DIM)


def body(queries, keys, values):
    tok_rows = queries.shape[0]
    back_blocks = WINDOW // tok_rows
    block_index = lax.axis_index(("blk", "grp"))
    pieces_k = []
    pieces_v = []
    for offset in range(back_blocks, 0, -1):
        moved_k, moved_v = from_behind((keys, values), ("blk", "grp"), offset)
        pieces_k.append(moved_k)
        pieces_v.append(moved_v)
    key_win = jnp.concatenate(pieces_k + [keys], axis=0)
    value_win = jnp.concatenate(pieces_v + [values], axis=0)
    return attend_block(queries, key_win, value_win, block_index)


def solution(mesh):
    placed = (P(("blk", "grp"), None), P(("blk", "grp"), None), P(("blk", "grp"), None))
    return jax.shard_map(
        body, mesh=mesh, in_specs=placed, out_specs=P(("blk", "grp"), None), check_vma=False
    )
```

profile of v0, /device:TPU:16, one launch (start us, length us, event | category | flops | bytes accessed | tf_op | source)
XLA Modules:
  0.0 158.4 jit_solution(14058204049214547418)
XLA Ops:
  0.0 1.3 copy.13
  1.3 3.4 %collective-permute-start = (bf16[256,1024]{0,1:T(8,128)(2,1)S(1)}, bf16[256,1024]{0,1:T(8,128)(2,1)}, u32[]{:S(2)}, u32[]{:S(2)}) collective-permute-start(bf16[256,1024]{0,1:T(8,128)(2,1)S(1)} %copy.13), channel_id=1, source_target_pairs={{0,4},{1,5},{2,6},{3,7},{4,8},{5,9},{6,10},{7,11},{8,12},{9,13},{1... | collective-permute-start | bytes 1572872 | tf_op jit(solution)/shard_map/ppermute | solution.py:15
  4.7 2.6 %collective-permute-start.1 = (bf16[256,1024]{0,1:T(8,128)(2,1)S(1)}, bf16[256,1024]{0,1:T(8,128)(2,1)}, u32[]{:S(2)}, u32[]{:S(2)}) collective-permute-start(bf16[256,1024]{0,1:T(8,128)(2,1)S(1)} %copy.13), channel_id=1, source_target_pairs={{0,3},{1,4},{2,5},{3,6},{4,7},{5,8},{6,9},{7,10},{8,11},{9,12},{10... | collective-permute-start | bytes 1572872 | tf_op jit(solution)/shard_map/ppermute | solution.py:15
  7.3 3.8 %collective-permute-start.2 = (bf16[256,1024]{0,1:T(8,128)(2,1)S(1)}, bf16[256,1024]{0,1:T(8,128)(2,1)}, u32[]{:S(2)}, u32[]{:S(2)}) collective-permute-start(bf16[256,1024]{0,1:T(8,128)(2,1)S(1)} %copy.13), channel_id=1, source_target_pairs={{0,2},{1,3},{2,4},{3,5},{4,6},{5,7},{6,8},{7,9},{8,10},{9,11},{10,... | collective-permute-start | bytes 1572872 | tf_op jit(solution)/shard_map/ppermute | solution.py:15
  11.1 2.3 %collective-permute-start.3 = (bf16[256,1024]{0,1:T(8,128)(2,1)S(1)}, bf16[256,1024]{0,1:T(8,128)(2,1)S(1)}, u32[]{:S(2)}, u32[]{:S(2)}) collective-permute-start(bf16[256,1024]{0,1:T(8,128)(2,1)S(1)} %copy.13), channel_id=1, source_target_pairs={{0,1},{1,2},{2,3},{3,4},{4,5},{5,6},{6,7},{7,8},{8,9},{9,10},{10,1... | collective-permute-start | bytes 1572872 | tf_op jit(solution)/shard_map/ppermute | solution.py:15
  13.5 3.4 %collective-permute-start.4 = (bf16[256,1024]{1,0:T(8,128)(2,1)}, bf16[256,1024]{1,0:T(8,128)(2,1)S(1)}, u32[]{:S(2)}, u32[]{:S(2)}) collective-permute-start(bf16[256,1024]{1,0:T(8,128)(2,1)} %param.6), channel_id=1, source_target_pairs={{0,4},{1,5},{2,6},{3,7},{4,8},{5,9},{6,10},{7,11},{8,12},{9,13},{1... | collective-permute-start | bytes 1572872 | tf_op jit(solution)/shard_map/ppermute | solution.py:15
  17.0 16.9 %collective-permute-done = bf16[256,1024]{0,1:T(8,128)(2,1)} collective-permute-done((bf16[256,1024]{0,1:T(8,128)(2,1)S(1)}, bf16[256,1024]{0,1:T(8,128)(2,1)}, u32[]{:S(2)}, u32[]{:S(2)}) %collective-permute-start) | collective-permute-done | bytes 524320 | tf_op jit(solution)/shard_map/ppermute | solution.py:15
  33.9 1.9 %collective-permute-start.5 = (bf16[256,1024]{1,0:T(8,128)(2,1)}, bf16[256,1024]{1,0:T(8,128)(2,1)S(1)}, u32[]{:S(2)}, u32[]{:S(2)}) collective-permute-start(bf16[256,1024]{1,0:T(8,128)(2,1)} %param.6), channel_id=1, source_target_pairs={{0,3},{1,4},{2,5},{3,6},{4,7},{5,8},{6,9},{7,10},{8,11},{9,12},{10... | collective-permute-start | bytes 1572872 | tf_op jit(solution)/shard_map/ppermute | solution.py:15
  35.8 1.1 constant_dynamic-update-slice_fusion.5
  36.9 0.7 collective-permute-done.1
  37.6 1.9 %collective-permute-start.6 = (bf16[256,1024]{1,0:T(8,128)(2,1)}, bf16[256,1024]{1,0:T(8,128)(2,1)S(1)}, u32[]{:S(2)}, u32[]{:S(2)}) collective-permute-start(bf16[256,1024]{1,0:T(8,128)(2,1)} %param.6), channel_id=1, source_target_pairs={{0,2},{1,3},{2,4},{3,5},{4,6},{5,7},{6,8},{7,9},{8,10},{9,11},{10,... | collective-permute-start | bytes 1572872 | tf_op jit(solution)/shard_map/ppermute | solution.py:15
  39.6 1.1 constant_dynamic-update-slice_fusion.4
  40.6 0.7 collective-permute-done.2
  41.4 6.2 %collective-permute-start.7 = (bf16[256,1024]{1,0:T(8,128)(2,1)S(1)}, bf16[256,1024]{1,0:T(8,128)(2,1)S(1)}, u32[]{:S(2)}, u32[]{:S(2)}) collective-permute-start(bf16[256,1024]{1,0:T(8,128)(2,1)S(1)} %copy-done), channel_id=1, source_target_pairs={{0,1},{1,2},{2,3},{3,4},{4,5},{5,6},{6,7},{7,8},{8,9},{9,10},{10,1... | collective-permute-start | bytes 1572872 | tf_op jit(solution)/shard_map/ppermute | solution.py:15
  47.6 1.1 constant_dynamic-update-slice_fusion.3
  48.7 11.8 %collective-permute-done.3 = bf16[256,1024]{0,1:T(8,128)(2,1)S(1)} collective-permute-done((bf16[256,1024]{0,1:T(8,128)(2,1)S(1)}, bf16[256,1024]{0,1:T(8,128)(2,1)S(1)}, u32[]{:S(2)}, u32[]{:S(2)}) %collective-permute-start.3) | collective-permute-done | bytes 524320 | tf_op jit(solution)/shard_map/ppermute | solution.py:15
  60.6 2.0 %collective-permute-done.5 = bf16[256,1024]{1,0:T(8,128)(2,1)S(1)} collective-permute-done((bf16[256,1024]{1,0:T(8,128)(2,1)}, bf16[256,1024]{1,0:T(8,128)(2,1)S(1)}, u32[]{:S(2)}, u32[]{:S(2)}) %collective-permute-start.5) | collective-permute-done | bytes 524320 | tf_op jit(solution)/shard_map/ppermute | solution.py:15
  62.6 1.2 collective-permute-done.6
  63.8 18.6 %collective-permute-done.7 = bf16[256,1024]{1,0:T(8,128)(2,1)S(1)} collective-permute-done((bf16[256,1024]{1,0:T(8,128)(2,1)S(1)}, bf16[256,1024]{1,0:T(8,128)(2,1)S(1)}, u32[]{:S(2)}, u32[]{:S(2)}) %collective-permute-start.7) | collective-permute-done | bytes 524320 | tf_op jit(solution)/shard_map/ppermute | solution.py:15
  82.5 1.5 copy-done.2
  84.0 72.9 %while.13 = (s32[]{:T(128)}, bf16[8,256,256]{1,2,0:T(8,128)(2,1)S(1)}, s32[8]{0:T(128)S(1)}, bf16[1280,1024]{0,1:T(8,128)(2,1)}, bf16[1280,1024]{1,0:T(8,128)(2,...) while((s32[]{:T(128)}, ...), condition=%wide.region_3.4_spmd.clone, body=%wide.region_0.3_spmd.clone.sunk | while | flops 341509376 | bytes 7936509 | solution.py:45
  85.2 0.9 constant_dynamic-slice_fusion.2
  87.1 3.7 %fusion.41 = (f32[2,256]{1,0:T(2,128)S(1)}, f32[2,256,1280]{1,2,0:T(8,128)}) fusion(bf16[256,2,128]{0,2,1:T(8,128)(2,1)S(1)} %bitcast.48, pred[256,1280]{0,1:T(8,128)(4,1)S(1)} %fusion.40, bf16[1280,1024]{1,0:T(8,128)(2,1)} %get-tuple-element.226, s32[]{:T(128)S(6)} %select_n.43), kind=kOutput, calls=%fused_computation.39.clone.1 | convolution fusion | flops 171050240 | bytes 3737604 | tf_op jit(solution)/shard_map/while/body/eval_jaxpr/sub | solution.py:39
  90.9 2.2 %fusion.42 = bf16[128,2,256]{2,0,1:T(8,128)(2,1)S(1)} fusion(f32[2,256,1280]{1,2,0:T(8,128)} %get-tuple-element.192, f32[2,256]{1,0:T(2,128)S(1)} %get-tuple-element.193, bf16[1280,1024]{0,1:T(8,128)(2,1)} %get-tuple-element.225, s32[]{:T(128)S(6)} %select_n.43), kind=kOutput, calls=%fused_computation.14.clone.1 | convolution fusion | flops 169148416 | bytes 3082244 | tf_op jit(solution)/shard_map/while/body/eval_jaxpr/htk,kd->thd/dot_general | solution.py:42
  94.3 0.9 constant_dynamic-slice_fusion.2
  96.2 3.7 %fusion.41 = (f32[2,256]{1,0:T(2,128)S(1)}, f32[2,256,1280]{1,2,0:T(8,128)}) fusion(bf16[256,2,128]{0,2,1:T(8,128)(2,1)S(1)} %bitcast.48, pred[256,1280]{0,1:T(8,128)(4,1)S(1)} %fusion.40, bf16[1280,1024]{1,0:T(8,128)(2,1)} %get-tuple-element.226, s32[]{:T(128)S(6)} %select_n.43), kind=kOutput, calls=%fused_computation.39.clone.1 | convolution fusion | flops 171050240 | bytes 3737604 | tf_op jit(solution)/shard_map/while/body/eval_jaxpr/sub | solution.py:39
  100.0 2.2 %fusion.42 = bf16[128,2,256]{2,0,1:T(8,128)(2,1)S(1)} fusion(f32[2,256,1280]{1,2,0:T(8,128)} %get-tuple-element.192, f32[2,256]{1,0:T(2,128)S(1)} %get-tuple-element.193, bf16[1280,1024]{0,1:T(8,128)(2,1)} %get-tuple-element.225, s32[]{:T(128)S(6)} %select_n.43), kind=kOutput, calls=%fused_computation.14.clone.1 | convolution fusion | flops 169148416 | bytes 3082244 | tf_op jit(solution)/shard_map/while/body/eval_jaxpr/htk,kd->thd/dot_general | solution.py:42
  102.2 0.6 dynamic_slice.51
  103.4 0.9 constant_dynamic-slice_fusion.2
  105.4 3.7 %fusion.41 = (f32[2,256]{1,0:T(2,128)S(1)}, f32[2,256,1280]{1,2,0:T(8,128)}) fusion(bf16[256,2,128]{0,2,1:T(8,128)(2,1)S(1)} %bitcast.48, pred[256,1280]{0,1:T(8,128)(4,1)S(1)} %fusion.40, bf16[1280,1024]{1,0:T(8,128)(2,1)} %get-tuple-element.226, s32[]{:T(128)S(6)} %select_n.43), kind=kOutput, calls=%fused_computation.39.clone.1 | convolution fusion | flops 171050240 | bytes 3737604 | tf_op jit(solution)/shard_map/while/body/eval_jaxpr/sub | solution.py:39
  109.1 2.2 %fusion.42 = bf16[128,2,256]{2,0,1:T(8,128)(2,1)S(1)} fusion(f32[2,256,1280]{1,2,0:T(8,128)} %get-tuple-element.192, f32[2,256]{1,0:T(2,128)S(1)} %get-tuple-element.193, bf16[1280,1024]{0,1:T(8,128)(2,1)} %get-tuple-element.225, s32[]{:T(128)S(6)} %select_n.43), kind=kOutput, calls=%fused_computation.14.clone.1 | convolution fusion | flops 169148416 | bytes 3082244 | tf_op jit(solution)/shard_map/while/body/eval_jaxpr/htk,kd->thd/dot_general | solution.py:42
  112.5 0.9 constant_dynamic-slice_fusion.2
  114.5 3.7 %fusion.41 = (f32[2,256]{1,0:T(2,128)S(1)}, f32[2,256,1280]{1,2,0:T(8,128)}) fusion(bf16[256,2,128]{0,2,1:T(8,128)(2,1)S(1)} %bitcast.48, pred[256,1280]{0,1:T(8,128)(4,1)S(1)} %fusion.40, bf16[1280,1024]{1,0:T(8,128)(2,1)} %get-tuple-element.226, s32[]{:T(128)S(6)} %select_n.43), kind=kOutput, calls=%fused_computation.39.clone.1 | convolution fusion | flops 171050240 | bytes 3737604 | tf_op jit(solution)/shard_map/while/body/eval_jaxpr/sub | solution.py:39
  118.2 2.2 %fusion.42 = bf16[128,2,256]{2,0,1:T(8,128)(2,1)S(1)} fusion(f32[2,256,1280]{1,2,0:T(8,128)} %get-tuple-element.192, f32[2,256]{1,0:T(2,128)S(1)} %get-tuple-element.193, bf16[1280,1024]{0,1:T(8,128)(2,1)} %get-tuple-element.225, s32[]{:T(128)S(6)} %select_n.43), kind=kOutput, calls=%fused_computation.14.clone.1 | convolution fusion | flops 169148416 | bytes 3082244 | tf_op jit(solution)/shard_map/while/body/eval_jaxpr/htk,kd->thd/dot_general | solution.py:42
  120.5 0.6 dynamic_slice.51
  121.6 0.9 constant_dynamic-slice_fusion.2
  123.6 3.7 %fusion.41 = (f32[2,256]{1,0:T(2,128)S(1)}, f32[2,256,1280]{1,2,0:T(8,128)}) fusion(bf16[256,2,128]{0,2,1:T(8,128)(2,1)S(1)} %bitcast.48, pred[256,1280]{0,1:T(8,128)(4,1)S(1)} %fusion.40, bf16[1280,1024]{1,0:T(8,128)(2,1)} %get-tuple-element.226, s32[]{:T(128)S(6)} %select_n.43), kind=kOutput, calls=%fused_computation.39.clone.1 | convolution fusion | flops 171050240 | bytes 3737604 | tf_op jit(solution)/shard_map/while/body/eval_jaxpr/sub | solution.py:39
  127.3 2.2 %fusion.42 = bf16[128,2,256]{2,0,1:T(8,128)(2,1)S(1)} fusion(f32[2,256,1280]{1,2,0:T(8,128)} %get-tuple-element.192, f32[2,256]{1,0:T(2,128)S(1)} %get-tuple-element.193, bf16[1280,1024]{0,1:T(8,128)(2,1)} %get-tuple-element.225, s32[]{:T(128)S(6)} %select_n.43), kind=kOutput, calls=%fused_computation.14.clone.1 | convolution fusion | flops 169148416 | bytes 3082244 | tf_op jit(solution)/shard_map/while/body/eval_jaxpr/htk,kd->thd/dot_general | solution.py:42
  130.8 0.9 constant_dynamic-slice_fusion.2
  132.7 3.7 %fusion.41 = (f32[2,256]{1,0:T(2,128)S(1)}, f32[2,256,1280]{1,2,0:T(8,128)}) fusion(bf16[256,2,128]{0,2,1:T(8,128)(2,1)S(1)} %bitcast.48, pred[256,1280]{0,1:T(8,128)(4,1)S(1)} %fusion.40, bf16[1280,1024]{1,0:T(8,128)(2,1)} %get-tuple-element.226, s32[]{:T(128)S(6)} %select_n.43), kind=kOutput, calls=%fused_computation.39.clone.1 | convolution fusion | flops 171050240 | bytes 3737604 | tf_op jit(solution)/shard_map/while/body/eval_jaxpr/sub | solution.py:39
  136.5 2.2 %fusion.42 = bf16[128,2,256]{2,0,1:T(8,128)(2,1)S(1)} fusion(f32[2,256,1280]{1,2,0:T(8,128)} %get-tuple-element.192, f32[2,256]{1,0:T(2,128)S(1)} %get-tuple-element.193, bf16[1280,1024]{0,1:T(8,128)(2,1)} %get-tuple-element.225, s32[]{:T(128)S(6)} %select_n.43), kind=kOutput, calls=%fused_computation.14.clone.1 | convolution fusion | flops 169148416 | bytes 3082244 | tf_op jit(solution)/shard_map/while/body/eval_jaxpr/htk,kd->thd/dot_general | solution.py:42
  139.9 0.9 constant_dynamic-slice_fusion.2
  141.8 3.7 %fusion.41 = (f32[2,256]{1,0:T(2,128)S(1)}, f32[2,256,1280]{1,2,0:T(8,128)}) fusion(bf16[256,2,128]{0,2,1:T(8,128)(2,1)S(1)} %bitcast.48, pred[256,1280]{0,1:T(8,128)(4,1)S(1)} %fusion.40, bf16[1280,1024]{1,0:T(8,128)(2,1)} %get-tuple-element.226, s32[]{:T(128)S(6)} %select_n.43), kind=kOutput, calls=%fused_computation.39.clone.1 | convolution fusion | flops 171050240 | bytes 3737604 | tf_op jit(solution)/shard_map/while/body/eval_jaxpr/sub | solution.py:39
  145.6 2.2 %fusion.42 = bf16[128,2,256]{2,0,1:T(8,128)(2,1)S(1)} fusion(f32[2,256,1280]{1,2,0:T(8,128)} %get-tuple-element.192, f32[2,256]{1,0:T(2,128)S(1)} %get-tuple-element.193, bf16[1280,1024]{0,1:T(8,128)(2,1)} %get-tuple-element.225, s32[]{:T(128)S(6)} %select_n.43), kind=kOutput, calls=%fused_computation.14.clone.1 | convolution fusion | flops 169148416 | bytes 3082244 | tf_op jit(solution)/shard_map/while/body/eval_jaxpr/htk,kd->thd/dot_general | solution.py:42
  149.0 0.9 constant_dynamic-slice_fusion.2
  151.0 3.7 %fusion.41 = (f32[2,256]{1,0:T(2,128)S(1)}, f32[2,256,1280]{1,2,0:T(8,128)}) fusion(bf16[256,2,128]{0,2,1:T(8,128)(2,1)S(1)} %bitcast.48, pred[256,1280]{0,1:T(8,128)(4,1)S(1)} %fusion.40, bf16[1280,1024]{1,0:T(8,128)(2,1)} %get-tuple-element.226, s32[]{:T(128)S(6)} %select_n.43), kind=kOutput, calls=%fused_computation.39.clone.1 | convolution fusion | flops 171050240 | bytes 3737604 | tf_op jit(solution)/shard_map/while/body/eval_jaxpr/sub | solution.py:39
  154.7 2.2 %fusion.42 = bf16[128,2,256]{2,0,1:T(8,128)(2,1)S(1)} fusion(f32[2,256,1280]{1,2,0:T(8,128)} %get-tuple-element.192, f32[2,256]{1,0:T(2,128)S(1)} %get-tuple-element.193, bf16[1280,1024]{0,1:T(8,128)(2,1)} %get-tuple-element.225, s32[]{:T(128)S(6)} %select_n.43), kind=kOutput, calls=%fused_computation.14.clone.1 | convolution fusion | flops 169148416 | bytes 3082244 | tf_op jit(solution)/shard_map/while/body/eval_jaxpr/htk,kd->thd/dot_general | solution.py:42
  156.9 1.4 copy.22
  (47 shorter events, 7.4 us)
Async XLA Ops:
  0.0 41.4 %copy-start = (bf16[256,1024]{1,0:T(8,128)(2,1)S(1)}, bf16[256,1024]{1,0:T(8,128)(2,1)}, u32[]{:S(2)}) copy-start(bf16[256,1024]{1,0:T(8,128)(2,1)} %param.6) | copy-start | bytes 1572868
  1.3 32.6 %collective-permute-start = (bf16[256,1024]{0,1:T(8,128)(2,1)S(1)}, bf16[256,1024]{0,1:T(8,128)(2,1)}, u32[]{:S(2)}, u32[]{:S(2)}) collective-permute-start(bf16[256,1024]{0,1:T(8,128)(2,1)S(1)} %copy.13), channel_id=1, source_target_pairs={{0,4},{1,5},{2,6},{3,7},{4,8},{5,9},{6,10},{7,11},{8,12},{9,13},{1... | collective-permute-start | bytes 1572872 | tf_op jit(solution)/shard_map/ppermute | solution.py:15
  4.7 32.9 %collective-permute-start.1 = (bf16[256,1024]{0,1:T(8,128)(2,1)S(1)}, bf16[256,1024]{0,1:T(8,128)(2,1)}, u32[]{:S(2)}, u32[]{:S(2)}) collective-permute-start(bf16[256,1024]{0,1:T(8,128)(2,1)S(1)} %copy.13), channel_id=1, source_target_pairs={{0,3},{1,4},{2,5},{3,6},{4,7},{5,8},{6,9},{7,10},{8,11},{9,12},{10... | collective-permute-start | bytes 1572872 | tf_op jit(solution)/shard_map/ppermute | solution.py:15
  7.3 34.1 %collective-permute-start.2 = (bf16[256,1024]{0,1:T(8,128)(2,1)S(1)}, bf16[256,1024]{0,1:T(8,128)(2,1)}, u32[]{:S(2)}, u32[]{:S(2)}) collective-permute-start(bf16[256,1024]{0,1:T(8,128)(2,1)S(1)} %copy.13), channel_id=1, source_target_pairs={{0,2},{1,3},{2,4},{3,5},{4,6},{5,7},{6,8},{7,9},{8,10},{9,11},{10,... | collective-permute-start | bytes 1572872 | tf_op jit(solution)/shard_map/ppermute | solution.py:15
  11.1 49.3 %collective-permute-start.3 = (bf16[256,1024]{0,1:T(8,128)(2,1)S(1)}, bf16[256,1024]{0,1:T(8,128)(2,1)S(1)}, u32[]{:S(2)}, u32[]{:S(2)}) collective-permute-start(bf16[256,1024]{0,1:T(8,128)(2,1)S(1)} %copy.13), channel_id=1, source_target_pairs={{0,1},{1,2},{2,3},{3,4},{4,5},{5,6},{6,7},{7,8},{8,9},{9,10},{10,1... | collective-permute-start | bytes 1572872 | tf_op jit(solution)/shard_map/ppermute | solution.py:15
  13.5 47.0 %collective-permute-start.4 = (bf16[256,1024]{1,0:T(8,128)(2,1)}, bf16[256,1024]{1,0:T(8,128)(2,1)S(1)}, u32[]{:S(2)}, u32[]{:S(2)}) collective-permute-start(bf16[256,1024]{1,0:T(8,128)(2,1)} %param.6), channel_id=1, source_target_pairs={{0,4},{1,5},{2,6},{3,7},{4,8},{5,9},{6,10},{7,11},{8,12},{9,13},{1... | collective-permute-start | bytes 1572872 | tf_op jit(solution)/shard_map/ppermute | solution.py:15
  33.9 28.7 %collective-permute-start.5 = (bf16[256,1024]{1,0:T(8,128)(2,1)}, bf16[256,1024]{1,0:T(8,128)(2,1)S(1)}, u32[]{:S(2)}, u32[]{:S(2)}) collective-permute-start(bf16[256,1024]{1,0:T(8,128)(2,1)} %param.6), channel_id=1, source_target_pairs={{0,3},{1,4},{2,5},{3,6},{4,7},{5,8},{6,9},{7,10},{8,11},{9,12},{10... | collective-permute-start | bytes 1572872 | tf_op jit(solution)/shard_map/ppermute | solution.py:15
  37.6 26.1 %collective-permute-start.6 = (bf16[256,1024]{1,0:T(8,128)(2,1)}, bf16[256,1024]{1,0:T(8,128)(2,1)S(1)}, u32[]{:S(2)}, u32[]{:S(2)}) collective-permute-start(bf16[256,1024]{1,0:T(8,128)(2,1)} %param.6), channel_id=1, source_target_pairs={{0,2},{1,3},{2,4},{3,5},{4,6},{5,7},{6,8},{7,9},{8,10},{9,11},{10,... | collective-permute-start | bytes 1572872 | tf_op jit(solution)/shard_map/ppermute | solution.py:15
  41.4 41.0 %collective-permute-start.7 = (bf16[256,1024]{1,0:T(8,128)(2,1)S(1)}, bf16[256,1024]{1,0:T(8,128)(2,1)S(1)}, u32[]{:S(2)}, u32[]{:S(2)}) collective-permute-start(bf16[256,1024]{1,0:T(8,128)(2,1)S(1)} %copy-done), channel_id=1, source_target_pairs={{0,1},{1,2},{2,3},{3,4},{4,5},{5,6},{6,7},{7,8},{8,9},{9,10},{10,1... | collective-permute-start | bytes 1572872 | tf_op jit(solution)/shard_map/ppermute | solution.py:15
  60.5 22.0 %copy-start.1 = (bf16[1280,1024]{0,1:T(8,128)(2,1)}, bf16[1280,1024]{0,1:T(8,128)(2,1)S(1)}, u32[]{:S(2)}) copy-start(bf16[1280,1024]{0,1:T(8,128)(2,1)S(1)} %constant_dynamic-update-slice_fusion.1) | copy-start | bytes 7864324
  82.5 1.5 copy-start.2
where the time goes:
time: 160 us; the launch traced here: 158 us
  waiting for transfers between devices  51.9 us (32%)
  matrix products  47.6 us (30%)
  starting transfers between devices  25.6 us (16%)
  local copies, waits for them, and re-layouts  20.7 us (13%)
  loops' own time  9.73 us (6%)
  other arithmetic  2.62 us (2%)
    ppermute x8, waiting for transfers between devices, from_behind(): return lax.ppermute(x, axis, pairs)  51.9 us
    sub x8, matrix products, head_group(): expo = jnp.where(allowed[None], jnp.exp(score - largest), jnp.float32(0.0))  29.9 us
    ppermute x8, starting transfers between devices, from_behind(): return lax.ppermute(x, axis, pairs)  25.6 us
    dot_general x8, matrix products, head_group(): jnp.einsum('htk,kd->thd', weight, value_part, preferred_element_type=jnp....  17.7 us
    another operation x1, loops' own time, attend_block(): parts = lax.map(head_group, jnp.arange(KV_HEADS, dtype=jnp.int32))  9.73 us
    dynamic_slice x16, local copies, waits for them, and re-layouts, head_group(): lax.dynamic_slice_in_dim(query_rows, head_index * group_size * HEAD_DIM,...  8.14 us
    unnamed x15, local copies, waits for them, and re-layouts  6.21 us
    dynamic_slice x8, local copies, waits for them, and re-layouts, attend_block(): parts = lax.map(head_group, jnp.arange(KV_HEADS, dtype=jnp.int32))  4.73 us
  transfers between devices with their start and end apart: 8, of which 7 were waited for; matrix products, arithmetic and copies ran while one was open for 2% of the time, Pallas kernels for 0%

commit v1 on v0

v1 whole, which is shorter than its diff:
```python
import functools

import jax
import jax.numpy as jnp
from jax import lax
from jax.experimental import pallas as pl
from jax.experimental.pallas import tpu as pltpu
from jax.sharding import PartitionSpec as P

HEADS = 16
KV_HEADS = 8
HEAD_DIM = 128
WINDOW = 1024
GROUP = HEADS // KV_HEADS
HALF_KV = KV_HEADS // 2
SLOTS = 7
SCALE_LOG2E = HEAD_DIM ** -0.5 * 1.4426950408889634
MESH = pl.DeviceIdType.MESH


def fused_kernel(
    rows, q_ref, k_ref, v_ref, o_ref, kv, other, qbuf, obuf,
    stage_sem, qstage_sem, qsend, qrecv, send, recv, osem, osend, orecv,
):
    blk = lax.axis_index("blk")
    side = lax.axis_index("grp")
    row = blk // 2
    core = blk % 2
    tok = q_ref.shape[0]
    has_prev = row > 0
    has_next = row < rows - 1
    own_slot = 4 + 2 * core

    partner = (2 * row + 1 - core, side)
    next_same = (2 * row + 2 + core, side)
    next_cross = (2 * row + 3 - core, side)
    side_same = (2 * row + core, 1 - side)
    side_cross = (2 * row + 1 - core, 1 - side)
    prev_same = (2 * row - 2 + core, side)
    prev_cross = (2 * row - 1 - core, side)

    def cols(index, width):
        return pl.ds(pl.multiple_of(index * width, width), width)

    def stage(j):
        mine = cols(core * HALF_KV + j, HEAD_DIM)
        rest = cols((1 - core) * HALF_KV + j, HEAD_DIM)
        return [
            pltpu.make_async_copy(k_ref.at[:, rest], other.at[j, 0], stage_sem.at[j, 0]),
            pltpu.make_async_copy(v_ref.at[:, rest], other.at[j, 1], stage_sem.at[j, 1]),
            pltpu.make_async_copy(k_ref.at[:, mine], kv.at[own_slot, j, 0], stage_sem.at[j, 2]),
            pltpu.make_async_copy(v_ref.at[:, mine], kv.at[own_slot, j, 1], stage_sem.at[j, 3]),
        ]

    def q_stage(j):
        mine = cols(core * HALF_KV + j, GROUP * HEAD_DIM)
        return pltpu.make_async_copy(q_ref.at[:, mine], qbuf.at[core, j], qstage_sem.at[j])

    def q_swap(j, block):
        rest = cols((1 - core) * HALF_KV + j, GROUP * HEAD_DIM)
        return pltpu.make_async_remote_copy(
            src_ref=q_ref.at[:, rest], dst_ref=qbuf.at[block, j],
            send_sem=qsend.at[j], recv_sem=qrecv.at[j], device_id=partner, device_id_type=MESH,
        )

    def remote(src, dst, kind, arrival, j, device):
        return pltpu.make_async_remote_copy(
            src_ref=src, dst_ref=dst, send_sem=send.at[kind, j], recv_sem=recv.at[arrival, j],
            device_id=device, device_id_type=MESH,
        )

    def to_partner(j):
        return remote(other.at[j], kv.at[own_slot, j], 0, own_slot, j, partner)

    def to_next(j):
        return [
            remote(kv.at[own_slot, j], kv.at[2 * core, j], 1, 2 * core, j, next_same),
            remote(other.at[j], kv.at[2 * core, j], 2, 2 * core, j, next_cross),
        ]

    def to_side(j):
        slot = jnp.where(side == 0, 3 + 2 * core, 5)
        return [
            remote(kv.at[own_slot, j], kv.at[slot, j], 3, slot, j, side_same),
            remote(other.at[j], kv.at[slot, j], 4, slot, j, side_cross),
        ]

    sends_side = jnp.logical_or(side == 0, core == 0)

    def pass_side_keys(j, slot, kind):
        return remote(kv.at[slot, j, 0], kv.at[1, j, 0], kind, 1, j, side_same)

    def pass_side_whole(j):
        return remote(kv.at[2, j], kv.at[3, j], 5, 3, j, side_same)

    def pass_next_values(j):
        return remote(kv.at[5, j, 1], kv.at[1, j, 1], 6, 7, j, next_same)

    def arrived(slot, j):
        remote(kv.at[slot, j], kv.at[slot, j], 0, slot, j, partner).wait_recv()

    def arrived_part(part, arrival, j):
        remote(kv.at[1, j, part], kv.at[1, j, part], 0, arrival, j, partner).wait_recv()

    def send_direct(j):
        for copy in stage(j):
            copy.wait()
        to_partner(j).start()

        @pl.when(sends_side)
        def _():
            for copy in to_side(j):
                copy.start()

        @pl.when(has_next)
        def _():
            for copy in to_next(j):
                copy.start()

    def forward(j):
        @pl.when(has_prev)
        def _():
            arrived(2, j)

            @pl.when(side == 1)
            def _():
                pass_side_whole(j).start()
                arrived(0, j)
                pass_side_keys(j, 0, 7).start()

            @pl.when(side == 0)
            def _():
                pass_side_keys(j, 2, 5).start()
                arrived(0, j)

        arrived(5, j)

        @pl.when(has_next)
        def _():
            pass_next_values(j).start()

    def await_rest(j):
        q_stage(j).wait()
        q_swap(j, 1 - core).wait_recv()
        arrived(6 - 2 * core, j)

        @pl.when(jnp.logical_or(side == 1, has_prev))
        def _():
            arrived(3, j)

        @pl.when(has_prev)
        def _():
            arrived_part(0, 1, j)
            arrived_part(1, 7, j)

    def attend(j, masked):
        upper = (
            lax.broadcasted_iota(jnp.int32, (tok, tok), 1) > lax.broadcasted_iota(jnp.int32, (tok, tok), 0)
        )

        def one_block(block, carry):
            base = 2 * block
            for h in range(GROUP):
                q = qbuf[block, j, :, h * HEAD_DIM:(h + 1) * HEAD_DIM]
                score = []
                for i in range(5):
                    s = lax.dot_general(
                        q, kv[base + i, j, 0], (((1,), (1,)), ((), ())), preferred_element_type=jnp.float32
                    )
                    if masked and i < 4:
                        s = jnp.where(4 * row + side + base + i >= 4, s, jnp.float32(-1e30))
                    score.append(s)
                score = [jnp.where(upper, score[0], score[4])] + score[1:4]
                top = jnp.max(jnp.maximum(jnp.maximum(score[0], score[1]), jnp.maximum(score[2], score[3])),
                              axis=1, keepdims=True)
                expo = [jnp.exp2((s - top) * jnp.float32(SCALE_LOG2E)) for s in score]
                total = jnp.sum((expo[0] + expo[1]) + (expo[2] + expo[3]), axis=1, keepdims=True)
                zero = jnp.zeros_like(expo[0])
                weight = [jnp.where(upper, expo[0], zero)] + expo[1:] + [jnp.where(upper, zero, expo[0])]
                out = None
                for i in range(5):
                    term = jnp.dot(
                        weight[i].astype(jnp.bfloat16), kv[base + i, j, 1], preferred_element_type=jnp.float32
                    )
                    out = term if out is None else out + term
                obuf[block, j, :, h * HEAD_DIM:(h + 1) * HEAD_DIM] = (out * (1.0 / total)).astype(obuf.dtype)
            return carry

        lax.fori_loop(0, 2, one_block, 0)

    def out_local(j):
        return pltpu.make_async_copy(
            obuf.at[core, j], o_ref.at[:, cols(core * HALF_KV + j, GROUP * HEAD_DIM)], osem.at[j]
        )

    def out_remote(j, half):
        return pltpu.make_async_remote_copy(
            src_ref=obuf.at[1 - core, j], dst_ref=o_ref.at[:, cols(half * HALF_KV + j, GROUP * HEAD_DIM)],
            send_sem=osend.at[j], recv_sem=orecv.at[j], device_id=partner, device_id_type=MESH,
        )

    for j in range(HALF_KV):
        for copy in stage(j):
            copy.start()
        q_stage(j).start()

    barrier = pltpu.get_barrier_semaphore()
    for device in (partner, side_same, side_cross):
        pl.semaphore_signal(barrier, inc=1, device_id=device, device_id_type=MESH)

    @pl.when(has_next)
    def _():
        for device in (next_same, next_cross):
            pl.semaphore_signal(barrier, inc=1, device_id=device, device_id_type=MESH)

    @pl.when(has_prev)
    def _():
        for device in (prev_same, prev_cross):
            pl.semaphore_signal(barrier, inc=1, device_id=device, device_id_type=MESH)

    @pl.when(jnp.logical_not(has_prev))
    def _():
        kv[0:3] = jnp.zeros((3,) + kv.shape[1:], kv.dtype)

        @pl.when(side == 0)
        def _():
            kv[3] = jnp.zeros(kv.shape[1:], kv.dtype)

    pl.semaphore_wait(barrier, 3 + jnp.where(has_next, 2, 0) + jnp.where(has_prev, 2, 0))

    send_direct(0)
    send_direct(1)
    for j in range(HALF_KV):
        q_swap(j, core).start()

    def step(t, carry):
        @pl.when(t < HALF_KV)
        def _():
            forward(t)

        @pl.when(t < HALF_KV - 2)
        def _():
            send_direct(t + 2)

        @pl.when(t > 0)
        def _():
            j = t - 1
            await_rest(j)

            @pl.when(has_prev)
            def _():
                attend(j, False)

            @pl.when(jnp.logical_not(has_prev))
            def _():
                attend(j, True)

            out_remote(j, core).start()
            out_local(j).start()

        return carry

    lax.fori_loop(0, HALF_KV + 1, step, 0)

    def finish(j, carry):
        q_swap(j, core).wait_send()
        to_partner(j).wait_send()

        @pl.when(sends_side)
        def _():
            for copy in to_side(j):
                copy.wait_send()

        @pl.when(has_next)
        def _():
            for copy in to_next(j):
                copy.wait_send()
            pass_next_values(j).wait_send()

        @pl.when(has_prev)
        def _():
            @pl.when(side == 1)
            def _():
                pass_side_whole(j).wait_send()
                pass_side_keys(j, 0, 7).wait_send()

            @pl.when(side == 0)
            def _():
                pass_side_keys(j, 2, 5).wait_send()

        out_local(j).wait()
        out_remote(j, core).wait_send()
        out_remote(j, 1 - core).wait_recv()
        return carry

    lax.fori_loop(0, HALF_KV, finish, 0)


def fused_body(rows, queries, keys, values):
    tok = queries.shape[0]
    kind = queries.dtype
    wide = GROUP * HEAD_DIM
    dma = pltpu.SemaphoreType.DMA
    return pl.pallas_call(
        functools.partial(fused_kernel, rows),
        out_shape=jax.ShapeDtypeStruct(queries.shape, kind),
        in_specs=[pl.BlockSpec(memory_space=pl.ANY)] * 3,
        out_specs=pl.BlockSpec(memory_space=pl.ANY),
        scratch_shapes=[
            pltpu.VMEM((SLOTS, HALF_KV, 2, tok, HEAD_DIM), kind),
            pltpu.VMEM((HALF_KV, 2, tok, HEAD_DIM), kind),
            pltpu.VMEM((2, HALF_KV, tok, wide), kind),
            pltpu.VMEM((2, HALF_KV, tok, wide), kind),
            dma((HALF_KV, 4)),
            dma((HALF_KV,)),
            dma((HALF_KV,)),
            dma((HALF_KV,)),
            dma((8, HALF_KV)),
            dma((8, HALF_KV)),
            dma((HALF_KV,)),
            dma((HALF_KV,)),
            dma((HALF_KV,)),
        ],
        compiler_params=pltpu.CompilerParams(
            collective_id=0, has_side_effects=True, vmem_limit_bytes=48 * 1024 * 1024
        ),
        cost_estimate=pl.CostEstimate(
            flops=4 * tok * HEADS * HEAD_DIM * (WINDOW + tok), bytes_accessed=6 * tok * HEADS * HEAD_DIM,
            transcendentals=tok * HEADS * WINDOW,
        ),
        name="window_attention",
    )(queries, keys, values)


def from_behind(x, axis, by):
    peers = lax.axis_size(axis)
    pairs = [(i, i + by) for i in range(peers) if 0 <= i + by < peers]
    return lax.ppermute(x, axis, pairs)


def attend_block(query_rows, key_win, value_win, block_index):
    tok_rows = query_rows.shape[0]
    span_rows = key_win.shape[0]
    row_ids = jnp.arange(tok_rows, dtype=jnp.int32)[:, None]
    col_ids = jnp.arange(span_rows, dtype=jnp.int32)[None, :]
    position = block_index * tok_rows - WINDOW + col_ids
    allowed = (col_ids > row_ids) & (col_ids <= row_ids + WINDOW) & (position >= 0)

    def head_group(head_index):
        query_part = lax.dynamic_slice_in_dim(query_rows, head_index * GROUP * HEAD_DIM, GROUP * HEAD_DIM, 1)
        query_part = query_part.reshape(tok_rows, GROUP, HEAD_DIM)
        key_part = lax.dynamic_slice_in_dim(key_win, head_index * HEAD_DIM, HEAD_DIM, 1)
        value_part = lax.dynamic_slice_in_dim(value_win, head_index * HEAD_DIM, HEAD_DIM, 1)
        score = jnp.einsum(
            "thd,kd->htk", query_part, key_part, preferred_element_type=jnp.float32
        ) * HEAD_DIM ** (-0.5)
        score = jnp.where(allowed[None], score, jnp.float32(-1e30))
        largest = jnp.max(score, axis=2, keepdims=True)
        expo = jnp.where(allowed[None], jnp.exp(score - largest), jnp.float32(0.0))
        total = jnp.sum(expo, axis=2, keepdims=True)
        weight = (expo / total).astype(jnp.bfloat16)
        output = jnp.einsum("htk,kd->thd", weight, value_part, preferred_element_type=jnp.float32)
        return output.astype(jnp.bfloat16).reshape(tok_rows, GROUP * HEAD_DIM)

    parts = lax.map(head_group, jnp.arange(KV_HEADS, dtype=jnp.int32))
    return jnp.transpose(parts, (1, 0, 2)).reshape(tok_rows, HEADS * HEAD_DIM)


def plain_body(queries, keys, values):
    back_blocks = WINDOW // queries.shape[0]
    block_index = lax.axis_index(("blk", "grp"))
    pieces_k = []
    pieces_v = []
    for offset in range(back_blocks, 0, -1):
        moved_k, moved_v = from_behind((keys, values), ("blk", "grp"), offset)
        pieces_k.append(moved_k)
        pieces_v.append(moved_v)
    key_win = jnp.concatenate(pieces_k + [keys], axis=0)
    value_win = jnp.concatenate(pieces_v + [values], axis=0)
    return attend_block(queries, key_win, value_win, block_index)


def solution(mesh):
    blks, grps = mesh.shape["blk"], mesh.shape["grp"]
    placed = P(("blk", "grp"), None)

    def body(queries, keys, values):
        if grps == 2 and blks % 2 == 0 and 4 * queries.shape[0] == WINDOW:
            return fused_body(blks // 2, queries, keys, values)
        return plain_body(queries, keys, values)

    return jax.shard_map(
        body, mesh=mesh, in_specs=(placed, placed, placed), out_specs=placed, check_vma=False
    )
```

time: 160 us -> 44.7 us (0.28)
  waiting for transfers between devices: 51.9 us -> 0 us
  matrix products: 47.6 us -> 0 us
  Pallas kernels: 0 us -> 39.6 us
  starting transfers between devices: 25.6 us -> 0 us
  local copies, waits for them, and re-layouts: 20.7 us -> 4.28 us
  loops' own time: 9.73 us -> 0 us
  other arithmetic: 2.62 us -> 0 us
    ppermute x8 -> x0, waiting for transfers between devices: 51.9 us -> none  [from_behind(): return lax.ppermute(x, axis, pairs)]
    pallas_call x0 -> x1, Pallas kernels: none -> 39.6 us  [fused_body(): pl.pallas_call(functools.partial(fused_kernel, rows), out_shape=jax.Shape...]
    sub x8 -> x0, matrix products: 29.9 us -> none  [head_group(): expo = jnp.where(allowed[None], jnp.exp(score - largest), jnp.float32(0.0))]
    ppermute x8 -> x0, starting transfers between devices: 25.6 us -> none  [from_behind(): return lax.ppermute(x, axis, pairs)]
    dot_general x8 -> x0, matrix products: 17.7 us -> none  [head_group(): jnp.einsum('htk,kd->thd', weight, value_part, preferred_element_type=jnp....]
    dynamic_slice x24 -> x0, local copies, waits for them, and re-layouts: 12.9 us -> none  [the longest x16 8.14 us: head_group(): lax.dynamic_slice_in_dim(query_rows, head_index * group_size * HEAD_DIM,...]
    another operation x1 -> x0, loops' own time: 9.73 us -> none  [attend_block(): parts = lax.map(head_group, jnp.arange(KV_HEADS, dtype=jnp.int32))]
    and x8 -> x0, other arithmetic: 2.61 us -> none  [attend_block(): (col_ids > row_ids) & (col_ids <= row_ids + WINDOW) & (position >= 0)]
  transfers between devices with their start and end apart: 8 -> 0, of which waited for: 7 -> 0; matrix products, arithmetic and copies ran while one was open for 2% -> 0% of each run, Pallas kernels for 0% -> 0%
where the time goes in v1:
time: 44.7 us; the launch traced here: 43.9 us
  Pallas kernels  39.6 us (89%)
  local copies, waits for them, and re-layouts  4.28 us (10%)
    pallas_call x1, Pallas kernels, fused_body(): pl.pallas_call(functools.partial(fused_kernel, rows), out_shape=jax.Shape...  39.6 us
    unnamed x7, local copies, waits for them, and re-layouts  4.28 us

profile of v1, /device:TPU:16, one launch (start us, length us, event | category | flops | bytes accessed | tf_op | source)
XLA Modules:
  0.0 43.9 jit_solution(13660444106725747318)
XLA Ops:
  0.0 0.0 copy-start
  0.0 1.2 %copy-done = bf16[256,2048]{1,0:T(8,128)(2,1)S(1)} copy-done((bf16[256,2048]{1,0:T(8,128)(2,1)S(1)}, bf16[256,2048]{1,0:T(8,128)(2,1)}, u32[]{:S(2)}) %copy-start) | copy-done | bytes 1048600
  1.2 0.0 copy-start.1
  1.2 1.0 %copy-done.1 = bf16[256,1024]{1,0:T(8,128)(2,1)S(1)} copy-done((bf16[256,1024]{1,0:T(8,128)(2,1)S(1)}, bf16[256,1024]{1,0:T(8,128)(2,1)}, u32[]{:S(2)}) %copy-start.1) | copy-done | bytes 524312
  2.3 0.0 copy-start.2
  2.3 1.0 %copy-done.2 = bf16[256,1024]{1,0:T(8,128)(2,1)S(1)} copy-done((bf16[256,1024]{1,0:T(8,128)(2,1)S(1)}, bf16[256,1024]{1,0:T(8,128)(2,1)}, u32[]{:S(2)}) %copy-start.2) | copy-done | bytes 524312
  3.3 39.6 %window_attention.1 = bf16[256,2048]{1,0:T(8,128)(2,1)S(1)} custom-call(bf16[256,2048]{1,0:T(8,128)(2,1)S(1)} %copy-done, bf16[256,1024]{1,0:T(8,128)(2,1)S(1)} %copy-done.1, bf16[256,1024]{1,0:T(8,128)(2,1)S(1)} %copy-done.2), custom_call_target="tpu_custom_call" | custom-call | flops 2684354560 | bytes 3145728 | tf_op jit(solution)/shard_map/window_attention/pallas_call | solution.py:304
  42.9 1.0 %copy.5 = bf16[256,2048]{1,0:T(8,128)(2,1)} copy(bf16[256,2048]{1,0:T(8,128)(2,1)S(1)} %window_attention.1) | data formatting | bytes 2097152
Async XLA Ops:
  0.0 1.2 %copy-start = (bf16[256,2048]{1,0:T(8,128)(2,1)S(1)}, bf16[256,2048]{1,0:T(8,128)(2,1)}, u32[]{:S(2)}) copy-start(bf16[256,2048]{1,0:T(8,128)(2,1)} %q_ref.1) | copy-start | bytes 3145732
  1.2 1.0 %copy-start.1 = (bf16[256,1024]{1,0:T(8,128)(2,1)S(1)}, bf16[256,1024]{1,0:T(8,128)(2,1)}, u32[]{:S(2)}) copy-start(bf16[256,1024]{1,0:T(8,128)(2,1)} %k_ref.1) | copy-start | bytes 1572868
  2.3 1.0 %copy-start.2 = (bf16[256,1024]{1,0:T(8,128)(2,1)S(1)}, bf16[256,1024]{1,0:T(8,128)(2,1)}, u32[]{:S(2)}) copy-start(bf16[256,1024]{1,0:T(8,128)(2,1)} %v_ref.1) | copy-start | bytes 1572868

commit v2 on v1

--- a/solution.py
+++ b/solution.py
@@ -42,15 +42,11 @@
     def cols(index, width):
         return pl.ds(pl.multiple_of(index * width, width), width)
 
-    def stage(j):
-        mine = cols(core * HALF_KV + j, HEAD_DIM)
-        rest = cols((1 - core) * HALF_KV + j, HEAD_DIM)
-        return [
-            pltpu.make_async_copy(k_ref.at[:, rest], other.at[j, 0], stage_sem.at[j, 0]),
-            pltpu.make_async_copy(v_ref.at[:, rest], other.at[j, 1], stage_sem.at[j, 1]),
-            pltpu.make_async_copy(k_ref.at[:, mine], kv.at[own_slot, j, 0], stage_sem.at[j, 2]),
-            pltpu.make_async_copy(v_ref.at[:, mine], kv.at[own_slot, j, 1], stage_sem.at[j, 3]),
-        ]
+    def stage(j, part, half):
+        source = (k_ref, v_ref)[part].at[:, cols(half * HALF_KV + j, HEAD_DIM)]
+        if half is core:
+            return pltpu.make_async_copy(source, kv.at[own_slot, j, part], stage_sem.at[j, 2 + part])
+        return pltpu.make_async_copy(source, other.at[j, part], stage_sem.at[j, part])
 
     def q_stage(j):
         mine = cols(core * HALF_KV + j, GROUP * HEAD_DIM)
@@ -63,95 +59,112 @@
             send_sem=qsend.at[j], recv_sem=qrecv.at[j], device_id=partner, device_id_type=MESH,
         )
 
-    def remote(src, dst, kind, arrival, j, device):
+    def remote(src, dst, kind, arrival, j, part, device):
         return pltpu.make_async_remote_copy(
-            src_ref=src, dst_ref=dst, send_sem=send.at[kind, j], recv_sem=recv.at[arrival, j],
+            src_ref=src, dst_ref=dst, send_sem=send.at[kind, j, part], recv_sem=recv.at[arrival, j, part],
             device_id=device, device_id_type=MESH,
         )
 
-    def to_partner(j):
-        return remote(other.at[j], kv.at[own_slot, j], 0, own_slot, j, partner)
-
-    def to_next(j):
+    def piece(slot, j, part):
+        return kv.at[slot, j, part]
+
+    def to_partner(j, part):
+        return remote(other.at[j, part], piece(own_slot, j, part), 0, own_slot, j, part, partner)
+
+    def to_next(j, part):
+        slot = 2 * core
         return [
-            remote(kv.at[own_slot, j], kv.at[2 * core, j], 1, 2 * core, j, next_same),
-            remote(other.at[j], kv.at[2 * core, j], 2, 2 * core, j, next_cross),
+            remote(piece(own_slot, j, part), piece(slot, j, part), 1, slot, j, part, next_same),
+            remote(other.at[j, part], piece(slot, j, part), 2, slot, j, part, next_cross),
         ]
 
-    def to_side(j):
+    def to_side(j, part):
         slot = jnp.where(side == 0, 3 + 2 * core, 5)
         return [
-            remote(kv.at[own_slot, j], kv.at[slot, j], 3, slot, j, side_same),
-            remote(other.at[j], kv.at[slot, j], 4, slot, j, side_cross),
+            remote(piece(own_slot, j, part), piece(slot, j, part), 3, slot, j, part, side_same),
+            remote(other.at[j, part], piece(slot, j, part), 4, slot, j, part, side_cross),
         ]
 
     sends_side = jnp.logical_or(side == 0, core == 0)
 
-    def pass_side_keys(j, slot, kind):
-        return remote(kv.at[slot, j, 0], kv.at[1, j, 0], kind, 1, j, side_same)
-
-    def pass_side_whole(j):
-        return remote(kv.at[2, j], kv.at[3, j], 5, 3, j, side_same)
-
-    def pass_next_values(j):
-        return remote(kv.at[5, j, 1], kv.at[1, j, 1], 6, 7, j, next_same)
-
-    def arrived(slot, j):
-        remote(kv.at[slot, j], kv.at[slot, j], 0, slot, j, partner).wait_recv()
-
-    def arrived_part(part, arrival, j):
-        remote(kv.at[1, j, part], kv.at[1, j, part], 0, arrival, j, partner).wait_recv()
-
-    def send_direct(j):
-        for copy in stage(j):
-            copy.wait()
-        to_partner(j).start()
+    def pass_side(j, part, slot, to_slot, kind):
+        return remote(piece(slot, j, part), piece(to_slot, j, part), kind, to_slot, j, part, side_same)
+
+    def pass_next(j):
+        return remote(piece(5, j, 1), piece(1, j, 1), 6, 1, j, 1, next_same)
+
+    def arrived(slot, j, part):
+        remote(piece(slot, j, part), piece(slot, j, part), 0, slot, j, part, partner).wait_recv()
+
+    def direct(j, part, act):
+        act(to_partner(j, part))
 
         @pl.when(sends_side)
         def _():
-            for copy in to_side(j):
+            for copy in to_side(j, part):
+                act(copy)
+
+        @pl.when(has_next)
+        def _():
+            for copy in to_next(j, part):
+                act(copy)
+
+    def forwards(j, part, act):
+        @pl.when(jnp.logical_and(has_prev, side == 1))
+        def _():
+            act(pass_side(j, part, 2, 3, 5), 2)
+            if part == 0:
+                act(pass_side(j, part, 0, 1, 7), 0)
+            else:
+                act(None, 0)
+
+        @pl.when(jnp.logical_and(has_prev, side == 0))
+        def _():
+            act(pass_side(j, part, 2, 1, 5) if part == 0 else None, 2)
+            act(None, 0)
+
+        if part == 0:
+            act(None, 5)
+        else:
+            @pl.when(has_next)
+            def _():
+                act(pass_next(j), 5)
+
+            @pl.when(jnp.logical_not(has_next))
+            def _():
+                act(None, 5)
+
+    def start_direct(j, part):
+        stage(j, part, core).wait()
+        stage(j, part, 1 - core).wait()
+        direct(j, part, lambda copy: copy.start())
+
+    def exchange(j, part):
+        def hand_on(copy, slot):
+            arrived(slot, j, part)
+            if copy is not None:
                 copy.start()
 
-        @pl.when(has_next)
-        def _():
-            for copy in to_next(j):
-                copy.start()
-
-    def forward(j):
-        @pl.when(has_prev)
-        def _():
-            arrived(2, j)
-
-            @pl.when(side == 1)
-            def _():
-                pass_side_whole(j).start()
-                arrived(0, j)
-                pass_side_keys(j, 0, 7).start()
-
-            @pl.when(side == 0)
-            def _():
-                pass_side_keys(j, 2, 5).start()
-                arrived(0, j)
-
-        arrived(5, j)
-
-        @pl.when(has_next)
-        def _():
-            pass_next_values(j).start()
+        forwards(j, part, hand_on)
+        direct(j, part, lambda copy: copy.wait_send())
+
+        @pl.when(j < HALF_KV - 1)
+        def _():
+            start_direct(j + 1, part)
 
     def await_rest(j):
         q_stage(j).wait()
         q_swap(j, 1 - core).wait_recv()
-        arrived(6 - 2 * core, j)
-
-        @pl.when(jnp.logical_or(side == 1, has_prev))
-        def _():
-            arrived(3, j)
-
-        @pl.when(has_prev)
-        def _():
-            arrived_part(0, 1, j)
-            arrived_part(1, 7, j)
+        for part in (0, 1):
+            arrived(6 - 2 * core, j, part)
+
+            @pl.when(jnp.logical_or(side == 1, has_prev))
+            def _():
+                arrived(3, j, part)
+
+            @pl.when(has_prev)
+            def _():
+                arrived(1, j, part)
 
     def attend(j, masked):
         upper = (
@@ -200,8 +213,9 @@
         )
 
     for j in range(HALF_KV):
-        for copy in stage(j):
-            copy.start()
+        for part in (0, 1):
+            stage(j, part, core).start()
+            stage(j, part, 1 - core).start()
         q_stage(j).start()
 
     barrier = pltpu.get_barrier_semaphore()
@@ -228,19 +242,16 @@
 
     pl.semaphore_wait(barrier, 3 + jnp.where(has_next, 2, 0) + jnp.where(has_prev, 2, 0))
 
-    send_direct(0)
-    send_direct(1)
+    start_direct(0, 0)
+    start_direct(0, 1)
     for j in range(HALF_KV):
         q_swap(j, core).start()
 
     def step(t, carry):
         @pl.when(t < HALF_KV)
         def _():
-            forward(t)
-
-        @pl.when(t < HALF_KV - 2)
-        def _():
-            send_direct(t + 2)
+            exchange(t, 0)
+            exchange(t, 1)
 
         @pl.when(t > 0)
         def _():
@@ -264,30 +275,8 @@
 
     def finish(j, carry):
         q_swap(j, core).wait_send()
-        to_partner(j).wait_send()
-
-        @pl.when(sends_side)
-        def _():
-            for copy in to_side(j):
-                copy.wait_send()
-
-        @pl.when(has_next)
-        def _():
-            for copy in to_next(j):
-                copy.wait_send()
-            pass_next_values(j).wait_send()
-
-        @pl.when(has_prev)
-        def _():
-            @pl.when(side == 1)
-            def _():
-                pass_side_whole(j).wait_send()
-                pass_side_keys(j, 0, 7).wait_send()
-
-            @pl.when(side == 0)
-            def _():
-                pass_side_keys(j, 2, 5).wait_send()
-
+        for part in (0, 1):
+            forwards(j, part, lambda copy, slot: None if copy is None else copy.wait_send())
         out_local(j).wait()
         out_remote(j, core).wait_send()
         out_remote(j, 1 - core).wait_recv()
@@ -315,14 +304,14 @@
             dma((HALF_KV,)),
             dma((HALF_KV,)),
             dma((HALF_KV,)),
-            dma((8, HALF_KV)),
-            dma((8, HALF_KV)),
+            dma((8, HALF_KV, 2)),
+            dma((SLOTS, HALF_KV, 2)),
             dma((HALF_KV,)),
             dma((HALF_KV,)),
             dma((HALF_KV,)),
         ],
         compiler_params=pltpu.CompilerParams(
-            collective_id=0, has_side_effects=True, vmem_limit_bytes=48 * 1024 * 1024
+            collective_id=0, has_side_effects=True, vmem_limit_bytes=62 * 1024 * 1024
         ),
         cost_estimate=pl.CostEstimate(
             flops=4 * tok * HEADS * HEAD_DIM * (WINDOW + tok), bytes_accessed=6 * tok * HEADS * HEAD_DIM,

time: 44.7 us -> 42.2 us (0.944)
  local copies, waits for them, and re-layouts: 4.28 us -> 2.3 us
    unnamed x7 -> x1, local copies, waits for them, and re-layouts: 4.28 us -> 2.3 us
where the time goes in v2:
time: 42.2 us; the launch traced here: 41.5 us
  Pallas kernels  39.2 us (93%)
  local copies, waits for them, and re-layouts  2.3 us (5%)
    pallas_call x1, Pallas kernels, fused_body(): pl.pallas_call(functools.partial(fused_kernel, rows), out_shape=jax.Shape...  39.2 us
    unnamed x1, local copies, waits for them, and re-layouts  2.3 us

profile of v2, /device:TPU:16, one launch (start us, length us, event | category | flops | bytes accessed | tf_op | source)
XLA Modules:
  0.0 41.5 jit_solution(16801597214340757751)
XLA Ops:
  0.0 39.2 %window_attention.1 = bf16[256,2048]{1,0:T(8,128)(2,1)} custom-call(bf16[256,2048]{1,0:T(8,128)(2,1)} %q_ref.1, bf16[256,1024]{1,0:T(8,128)(2,1)} %k_ref.1, bf16[256,1024]{1,0:T(8,128)(2,1)} %v_ref.1), custom_call_target="tpu_custom_call" | custom-call | flops 2684354560 | bytes 3145728 | tf_op jit(solution)/shard_map/window_attention/pallas_call | solution.py:293
  39.2 2.3 %copy.5 = bf16[256,2048]{1,0:T(8,128)(2,1)} copy(bf16[256,2048]{1,0:T(8,128)(2,1)} %window_attention.1) | data formatting | bytes 2097152

commit v3 on v2

--- a/solution.py
+++ b/solution.py
@@ -19,7 +19,7 @@
 
 
 def fused_kernel(
-    rows, q_ref, k_ref, v_ref, o_ref, kv, other, qbuf, obuf,
+    rows, q_ref, k_ref, v_ref, o_ref, kv, other, qbuf, wbuf, obuf,
     stage_sem, qstage_sem, qsend, qrecv, send, recv, osem, osend, orecv,
 ):
     blk = lax.axis_index("blk")
@@ -96,13 +96,14 @@
     def arrived(slot, j, part):
         remote(piece(slot, j, part), piece(slot, j, part), 0, slot, j, part, partner).wait_recv()
 
-    def direct(j, part, act):
-        act(to_partner(j, part))
-
+    def direct_side(j, part, act):
         @pl.when(sends_side)
         def _():
             for copy in to_side(j, part):
                 act(copy)
+
+    def direct_next(j, part, act):
+        act(to_partner(j, part))
 
         @pl.when(has_next)
         def _():
@@ -134,10 +135,17 @@
             def _():
                 act(None, 5)
 
+    def launch(copy):
+        copy.start()
+
+    def sent(copy):
+        copy.wait_send()
+
     def start_direct(j, part):
         stage(j, part, core).wait()
         stage(j, part, 1 - core).wait()
-        direct(j, part, lambda copy: copy.start())
+        direct_side(j, part, launch)
+        direct_next(j, part, launch)
 
     def exchange(j, part):
         def hand_on(copy, slot):
@@ -146,27 +154,45 @@
                 copy.start()
 
         forwards(j, part, hand_on)
-        direct(j, part, lambda copy: copy.wait_send())
-
-        @pl.when(j < HALF_KV - 1)
-        def _():
-            start_direct(j + 1, part)
-
-    def await_rest(j):
+        direct_side(j, part, sent)
+        direct_next(j, part, sent)
+
+        @pl.when(j < HALF_KV - 1 - part)
+        def _():
+            start_direct(j + 1 + part, 1 - part)
+
+    def arrived_rest(j, part):
+        arrived(6 - 2 * core, j, part)
+
+        @pl.when(jnp.logical_or(side == 1, has_prev))
+        def _():
+            arrived(3, j, part)
+
+        @pl.when(has_prev)
+        def _():
+            arrived(1, j, part)
+
+    def weigh_chunk(j):
         q_stage(j).wait()
         q_swap(j, 1 - core).wait_recv()
-        for part in (0, 1):
-            arrived(6 - 2 * core, j, part)
-
-            @pl.when(jnp.logical_or(side == 1, has_prev))
-            def _():
-                arrived(3, j, part)
-
-            @pl.when(has_prev)
-            def _():
-                arrived(1, j, part)
-
-    def attend(j, masked):
+        arrived_rest(j, 0)
+
+        @pl.when(has_prev)
+        def _():
+            weigh(j, False)
+
+        @pl.when(jnp.logical_not(has_prev))
+        def _():
+            weigh(j, True)
+
+    def blend_chunk(j):
+        arrived_rest(j, 1)
+        blend(j, 1 - core)
+        out_remote(j, core).start()
+        blend(j, core)
+        out_local(j).start()
+
+    def weigh(j, masked):
         upper = (
             lax.broadcasted_iota(jnp.int32, (tok, tok), 1) > lax.broadcasted_iota(jnp.int32, (tok, tok), 0)
         )
@@ -188,18 +214,25 @@
                               axis=1, keepdims=True)
                 expo = [jnp.exp2((s - top) * jnp.float32(SCALE_LOG2E)) for s in score]
                 total = jnp.sum((expo[0] + expo[1]) + (expo[2] + expo[3]), axis=1, keepdims=True)
+                share = 1.0 / total
+                expo = [e * share for e in expo]
                 zero = jnp.zeros_like(expo[0])
                 weight = [jnp.where(upper, expo[0], zero)] + expo[1:] + [jnp.where(upper, zero, expo[0])]
-                out = None
                 for i in range(5):
-                    term = jnp.dot(
-                        weight[i].astype(jnp.bfloat16), kv[base + i, j, 1], preferred_element_type=jnp.float32
-                    )
-                    out = term if out is None else out + term
-                obuf[block, j, :, h * HEAD_DIM:(h + 1) * HEAD_DIM] = (out * (1.0 / total)).astype(obuf.dtype)
+                    wbuf[block, i, h * tok:(h + 1) * tok, :] = weight[i].astype(wbuf.dtype)
             return carry
 
         lax.fori_loop(0, 2, one_block, 0)
+
+    def blend(j, block):
+        base = 2 * block
+        out = None
+        for i in range(5):
+            term = jnp.dot(wbuf[block, i], kv[base + i, j, 1], preferred_element_type=jnp.float32)
+            out = term if out is None else out + term
+        out = out.astype(obuf.dtype)
+        for h in range(GROUP):
+            obuf[block, j, :, h * HEAD_DIM:(h + 1) * HEAD_DIM] = out[h * tok:(h + 1) * tok]
 
     def out_local(j):
         return pltpu.make_async_copy(
@@ -243,31 +276,24 @@
     pl.semaphore_wait(barrier, 3 + jnp.where(has_next, 2, 0) + jnp.where(has_prev, 2, 0))
 
     start_direct(0, 0)
-    start_direct(0, 1)
     for j in range(HALF_KV):
         q_swap(j, core).start()
-
-    def step(t, carry):
-        @pl.when(t < HALF_KV)
-        def _():
-            exchange(t, 0)
-            exchange(t, 1)
-
-        @pl.when(t > 0)
-        def _():
-            j = t - 1
-            await_rest(j)
-
-            @pl.when(has_prev)
-            def _():
-                attend(j, False)
-
-            @pl.when(jnp.logical_not(has_prev))
-            def _():
-                attend(j, True)
-
-            out_remote(j, core).start()
-            out_local(j).start()
+    start_direct(0, 1)
+    start_direct(1, 0)
+
+    def step(j, carry):
+        @pl.when(j < HALF_KV)
+        def _():
+            exchange(j, 0)
+
+        @pl.when(j > 0)
+        def _():
+            blend_chunk(j - 1)
+
+        @pl.when(j < HALF_KV)
+        def _():
+            exchange(j, 1)
+            weigh_chunk(j)
 
         return carry
 
@@ -299,6 +325,7 @@
             pltpu.VMEM((SLOTS, HALF_KV, 2, tok, HEAD_DIM), kind),
             pltpu.VMEM((HALF_KV, 2, tok, HEAD_DIM), kind),
             pltpu.VMEM((2, HALF_KV, tok, wide), kind),
+            pltpu.VMEM((2, 5, GROUP * tok, tok), kind),
             pltpu.VMEM((2, HALF_KV, tok, wide), kind),
             dma((HALF_KV, 4)),
             dma((HALF_KV,)),
@@ -311,7 +338,7 @@
             dma((HALF_KV,)),
         ],
         compiler_params=pltpu.CompilerParams(
-            collective_id=0, has_side_effects=True, vmem_limit_bytes=62 * 1024 * 1024
+            collective_id=0, has_side_effects=True, vmem_limit_bytes=58 * 1024 * 1024
         ),
         cost_estimate=pl.CostEstimate(
             flops=4 * tok * HEADS * HEAD_DIM * (WINDOW + tok), bytes_accessed=6 * tok * HEADS * HEAD_DIM,

time: 42.2 us -> 42.4 us (level); the launches traced: 41.5 us -> 42.1 us
  Pallas kernels: 39.2 us -> 39.8 us
    pallas_call x1, Pallas kernels: 39.2 us -> 39.8 us  [fused_body(): pl.pallas_call(functools.partial(fused_kernel, rows), out_shape=jax.Shape...]
where the time goes in v3:
time: 42.4 us; the launch traced here: 42.1 us
  Pallas kernels  39.8 us (94%)
  local copies, waits for them, and re-layouts  2.3 us (5%)
    pallas_call x1, Pallas kernels, fused_body(): pl.pallas_call(functools.partial(fused_kernel, rows), out_shape=jax.Shape...  39.8 us
    unnamed x1, local copies, waits for them, and re-layouts  2.3 us

profile of v3, /device:TPU:16, one launch (start us, length us, event | category | flops | bytes accessed | tf_op | source)
XLA Modules:
  0.0 42.1 jit_solution(809295689383360797)
XLA Ops:
  0.0 39.8 %window_attention.1 = bf16[256,2048]{1,0:T(8,128)(2,1)} custom-call(bf16[256,2048]{1,0:T(8,128)(2,1)} %q_ref.1, bf16[256,1024]{1,0:T(8,128)(2,1)} %k_ref.1, bf16[256,1024]{1,0:T(8,128)(2,1)} %v_ref.1), custom_call_target="tpu_custom_call" | custom-call | flops 2684354560 | bytes 3145728 | tf_op jit(solution)/shard_map/window_attention/pallas_call | solution.py:319
  39.8 2.3 %copy.5 = bf16[256,2048]{1,0:T(8,128)(2,1)} copy(bf16[256,2048]{1,0:T(8,128)(2,1)} %window_attention.1) | data formatting | bytes 2097152

commit v4 on v3

--- a/solution.py
+++ b/solution.py
@@ -141,11 +141,9 @@
     def sent(copy):
         copy.wait_send()
 
-    def start_direct(j, part):
+    def staged(j, part):
         stage(j, part, core).wait()
         stage(j, part, 1 - core).wait()
-        direct_side(j, part, launch)
-        direct_next(j, part, launch)
 
     def exchange(j, part):
         def hand_on(copy, slot):
@@ -159,7 +157,15 @@
 
         @pl.when(j < HALF_KV - 1 - part)
         def _():
-            start_direct(j + 1 + part, 1 - part)
+            direct_next(j + 1 + part, 1 - part, launch)
+
+        @pl.when(jnp.logical_and(side == 0, j < HALF_KV - 1 - part))
+        def _():
+            direct_side(j + 1 + part, 1 - part, launch)
+
+        @pl.when(jnp.logical_and(side == 1, j < HALF_KV - 2 - part))
+        def _():
+            direct_side(j + 2 + part, 1 - part, launch)
 
     def arrived_rest(j, part):
         arrived(6 - 2 * core, j, part)
@@ -275,11 +281,21 @@
 
     pl.semaphore_wait(barrier, 3 + jnp.where(has_next, 2, 0) + jnp.where(has_prev, 2, 0))
 
-    start_direct(0, 0)
-    for j in range(HALF_KV):
-        q_swap(j, core).start()
-    start_direct(0, 1)
-    start_direct(1, 0)
+    for j, part in ((0, 0), (0, 1), (1, 0)):
+        staged(j, part)
+        direct_next(j, part, launch)
+        direct_side(j, part, launch)
+        if part == 0:
+            q_swap(j, core).start()
+    for j, part in ((1, 1), (2, 0), (2, 1), (3, 0), (3, 1)):
+        staged(j, part)
+        if part == 0:
+            q_swap(j, core).start()
+
+    @pl.when(side == 1)
+    def _():
+        direct_side(1, 1, launch)
+        direct_side(2, 0, launch)
 
     def step(j, carry):
         @pl.when(j < HALF_KV)
@@ -288,12 +304,15 @@
 
         @pl.when(j > 0)
         def _():
+            weigh_chunk(j - 1)
+
+        @pl.when(j < HALF_KV)
+        def _():
+            exchange(j, 1)
+
+        @pl.when(j > 0)
+        def _():
             blend_chunk(j - 1)
-
-        @pl.when(j < HALF_KV)
-        def _():
-            exchange(j, 1)
-            weigh_chunk(j)
 
         return carry
 

time: 42.4 us -> 40.5 us (0.955)
  Pallas kernels: 39.8 us -> 37.9 us
    pallas_call x1, Pallas kernels: 39.8 us -> 37.9 us  [fused_body(): pl.pallas_call(functools.partial(fused_kernel, rows), out_shape=jax.Shape...]
where the time goes in v4:
time: 40.5 us; the launch traced here: 40.2 us
  Pallas kernels  37.9 us (94%)
  local copies, waits for them, and re-layouts  2.3 us (6%)
    pallas_call x1, Pallas kernels, fused_body(): pl.pallas_call(functools.partial(fused_kernel, rows), out_shape=jax.Shape...  37.9 us
    unnamed x1, local copies, waits for them, and re-layouts  2.3 us

profile of v4, /device:TPU:16, one launch (start us, length us, event | category | flops | bytes accessed | tf_op | source)
XLA Modules:
  0.0 40.2 jit_solution(10587405286432312525)
XLA Ops:
  0.0 37.9 %window_attention.1 = bf16[256,2048]{1,0:T(8,128)(2,1)} custom-call(bf16[256,2048]{1,0:T(8,128)(2,1)} %q_ref.1, bf16[256,1024]{1,0:T(8,128)(2,1)} %k_ref.1, bf16[256,1024]{1,0:T(8,128)(2,1)} %v_ref.1), custom_call_target="tpu_custom_call" | custom-call | flops 2684354560 | bytes 3145728 | tf_op jit(solution)/shard_map/window_attention/pallas_call | solution.py:338
  37.9 2.3 %copy.5 = bf16[256,2048]{1,0:T(8,128)(2,1)} copy(bf16[256,2048]{1,0:T(8,128)(2,1)} %window_attention.1) | data formatting | bytes 2097152

commit v5 on v4

--- a/solution.py
+++ b/solution.py
@@ -14,12 +14,13 @@
 GROUP = HEADS // KV_HEADS
 HALF_KV = KV_HEADS // 2
 SLOTS = 7
+TILE = 16
 SCALE_LOG2E = HEAD_DIM ** -0.5 * 1.4426950408889634
 MESH = pl.DeviceIdType.MESH
 
 
 def fused_kernel(
-    rows, q_ref, k_ref, v_ref, o_ref, kv, other, qbuf, wbuf, obuf,
+    rows, q_ref, k_ref, v_ref, o_ref, kv, other, qbuf, sbuf, wbuf, obuf,
     stage_sem, qstage_sem, qsend, qrecv, send, recv, osem, osend, orecv,
 ):
     blk = lax.axis_index("blk")
@@ -183,13 +184,7 @@
         q_swap(j, 1 - core).wait_recv()
         arrived_rest(j, 0)
 
-        @pl.when(has_prev)
-        def _():
-            weigh(j, False)
-
-        @pl.when(jnp.logical_not(has_prev))
-        def _():
-            weigh(j, True)
+        weigh(j)
 
     def blend_chunk(j):
         arrived_rest(j, 1)
@@ -198,37 +193,41 @@
         blend(j, core)
         out_local(j).start()
 
-    def weigh(j, masked):
-        upper = (
-            lax.broadcasted_iota(jnp.int32, (tok, tok), 1) > lax.broadcasted_iota(jnp.int32, (tok, tok), 0)
-        )
-
-        def one_block(block, carry):
+    def weigh(j):
+        for unit in range(2 * GROUP):
+            block, h = unit // GROUP, unit % GROUP
             base = 2 * block
-            for h in range(GROUP):
-                q = qbuf[block, j, :, h * HEAD_DIM:(h + 1) * HEAD_DIM]
-                score = []
-                for i in range(5):
-                    s = lax.dot_general(
-                        q, kv[base + i, j, 0], (((1,), (1,)), ((), ())), preferred_element_type=jnp.float32
-                    )
-                    if masked and i < 4:
-                        s = jnp.where(4 * row + side + base + i >= 4, s, jnp.float32(-1e30))
-                    score.append(s)
-                score = [jnp.where(upper, score[0], score[4])] + score[1:4]
-                top = jnp.max(jnp.maximum(jnp.maximum(score[0], score[1]), jnp.maximum(score[2], score[3])),
-                              axis=1, keepdims=True)
-                expo = [jnp.exp2((s - top) * jnp.float32(SCALE_LOG2E)) for s in score]
-                total = jnp.sum((expo[0] + expo[1]) + (expo[2] + expo[3]), axis=1, keepdims=True)
-                share = 1.0 / total
-                expo = [e * share for e in expo]
-                zero = jnp.zeros_like(expo[0])
-                weight = [jnp.where(upper, expo[0], zero)] + expo[1:] + [jnp.where(upper, zero, expo[0])]
-                for i in range(5):
-                    wbuf[block, i, h * tok:(h + 1) * tok, :] = weight[i].astype(wbuf.dtype)
-            return carry
-
-        lax.fori_loop(0, 2, one_block, 0)
+            score = sbuf.at[unit % 2]
+            q = qbuf[block, j, :, h * HEAD_DIM:(h + 1) * HEAD_DIM]
+            upper = (
+                lax.broadcasted_iota(jnp.int32, (tok, tok), 1) > lax.broadcasted_iota(jnp.int32, (tok, tok), 0)
+            )
+            for i in (4, 0, 1, 2, 3):
+                s = lax.dot_general(
+                    q, kv[base + i, j, 0], (((1,), (1,)), ((), ())), preferred_element_type=jnp.float32
+                )
+                if i == 4:
+                    last = s
+                    continue
+                s = jnp.where(4 * row + side + base + i >= 4, s, jnp.float32(-1e30))
+                if i == 0:
+                    s = jnp.where(upper, s, last)
+                score[:, i * tok:(i + 1) * tok] = s
+            for r in range(0, tok, TILE):
+                part = score[r:r + TILE, :]
+                top = jnp.max(part, axis=1, keepdims=True)
+                expo = jnp.exp2((part - top) * jnp.float32(SCALE_LOG2E))
+                weight = expo * (1.0 / jnp.sum(expo, axis=1, keepdims=True))
+                rows_here = slice(h * tok + r, h * tok + r + TILE)
+                first = weight[:, :tok]
+                ahead = (
+                    lax.broadcasted_iota(jnp.int32, (TILE, tok), 1)
+                    > lax.broadcasted_iota(jnp.int32, (TILE, tok), 0) + r
+                )
+                wbuf[block, 0, rows_here, :] = jnp.where(ahead, first, 0.0).astype(wbuf.dtype)
+                wbuf[block, 4, rows_here, :] = jnp.where(ahead, 0.0, first).astype(wbuf.dtype)
+                for i in range(1, 4):
+                    wbuf[block, i, rows_here, :] = weight[:, i * tok:(i + 1) * tok].astype(wbuf.dtype)
 
     def blend(j, block):
         base = 2 * block
@@ -344,6 +343,7 @@
             pltpu.VMEM((SLOTS, HALF_KV, 2, tok, HEAD_DIM), kind),
             pltpu.VMEM((HALF_KV, 2, tok, HEAD_DIM), kind),
             pltpu.VMEM((2, HALF_KV, tok, wide), kind),
+            pltpu.VMEM((2, tok, WINDOW), jnp.float32),
             pltpu.VMEM((2, 5, GROUP * tok, tok), kind),
             pltpu.VMEM((2, HALF_KV, tok, wide), kind),
             dma((HALF_KV, 4)),

time: 40.5 us -> 40.5 us (level)
  no operation moved by 1% of the time
where the time goes in v5:
time: 40.5 us; the launch traced here: 40.2 us
  Pallas kernels  37.9 us (94%)
  local copies, waits for them, and re-layouts  2.3 us (6%)
    pallas_call x1, Pallas kernels, fused_body(): pl.pallas_call(functools.partial(fused_kernel, rows), out_shape=jax.Shape...  37.9 us
    unnamed x1, local copies, waits for them, and re-layouts  2.3 us

profile of v5, /device:TPU:16, one launch (start us, length us, event | category | flops | bytes accessed | tf_op | source)
XLA Modules:
  0.0 40.2 jit_solution(11244330659431232726)
XLA Ops:
  0.0 37.9 %window_attention.1 = bf16[256,2048]{1,0:T(8,128)(2,1)} custom-call(bf16[256,2048]{1,0:T(8,128)(2,1)} %q_ref.1, bf16[256,1024]{1,0:T(8,128)(2,1)} %k_ref.1, bf16[256,1024]{1,0:T(8,128)(2,1)} %v_ref.1), custom_call_target="tpu_custom_call" | custom-call | flops 2684354560 | bytes 3145728 | tf_op jit(solution)/shard_map/window_attention/pallas_call | solution.py:337
  37.9 2.3 %copy.5 = bf16[256,2048]{1,0:T(8,128)(2,1)} copy(bf16[256,2048]{1,0:T(8,128)(2,1)} %window_attention.1) | data formatting | bytes 2097152

commit v6 on v5

--- a/solution.py
+++ b/solution.py
@@ -15,6 +15,8 @@
 HALF_KV = KV_HEADS // 2
 SLOTS = 7
 TILE = 16
+TURNS = 2 * HALF_KV
+DEPTH = 3
 SCALE_LOG2E = HEAD_DIM ** -0.5 * 1.4426950408889634
 MESH = pl.DeviceIdType.MESH
 
@@ -112,29 +114,34 @@
                 act(copy)
 
     def forwards(j, part, act):
+        @pl.when(jnp.logical_and(has_prev, jnp.logical_and(side == 1, part == 0)))
+        def _():
+            act(pass_side(j, part, 0, 1, 7), 0)
+
         @pl.when(jnp.logical_and(has_prev, side == 1))
         def _():
             act(pass_side(j, part, 2, 3, 5), 2)
-            if part == 0:
-                act(pass_side(j, part, 0, 1, 7), 0)
-            else:
-                act(None, 0)
-
-        @pl.when(jnp.logical_and(has_prev, side == 0))
-        def _():
-            act(pass_side(j, part, 2, 1, 5) if part == 0 else None, 2)
-            act(None, 0)
-
-        if part == 0:
-            act(None, 5)
-        else:
-            @pl.when(has_next)
-            def _():
-                act(pass_next(j), 5)
-
-            @pl.when(jnp.logical_not(has_next))
-            def _():
-                act(None, 5)
+
+        @pl.when(jnp.logical_and(has_prev, jnp.logical_and(side == 0, part == 0)))
+        def _():
+            act(pass_side(j, part, 2, 1, 5), 2)
+
+        @pl.when(jnp.logical_and(has_next, part == 1))
+        def _():
+            act(pass_next(j), 5)
+
+    def await_kept(j, part):
+        @pl.when(jnp.logical_and(has_prev, jnp.logical_or(side == 0, part == 1)))
+        def _():
+            arrived(0, j, part)
+
+        @pl.when(jnp.logical_and(has_prev, jnp.logical_and(side == 0, part == 1)))
+        def _():
+            arrived(2, j, part)
+
+        @pl.when(jnp.logical_not(jnp.logical_and(has_next, part == 1)))
+        def _():
+            arrived(5, j, part)
 
     def launch(copy):
         copy.start()
@@ -146,27 +153,38 @@
         stage(j, part, core).wait()
         stage(j, part, 1 - core).wait()
 
-    def exchange(j, part):
+    def turn(t):
+        first, last, odd = t == 0, t == TURNS - 1, t % 2 == 1
+        part = jnp.where(first, 0, jnp.where(last, 1, 1 - t % 2))
+        return jnp.where(first, 0, jnp.where(last, HALF_KV - 1, jnp.where(odd, (t + 1) // 2, t // 2 - 1))), part
+
+    def start_next(t):
+        j, part = turn(t)
+        direct_next(j, part, launch)
+
+        @pl.when(side == 0)
+        def _():
+            direct_side(j, part, launch)
+
+    def exchange(t):
+        j, part = turn(t)
+
         def hand_on(copy, slot):
             arrived(slot, j, part)
-            if copy is not None:
-                copy.start()
+            copy.start()
 
         forwards(j, part, hand_on)
-        direct_side(j, part, sent)
-        direct_next(j, part, sent)
-
-        @pl.when(j < HALF_KV - 1 - part)
-        def _():
-            direct_next(j + 1 + part, 1 - part, launch)
-
-        @pl.when(jnp.logical_and(side == 0, j < HALF_KV - 1 - part))
-        def _():
-            direct_side(j + 1 + part, 1 - part, launch)
-
-        @pl.when(jnp.logical_and(side == 1, j < HALF_KV - 2 - part))
-        def _():
-            direct_side(j + 2 + part, 1 - part, launch)
+        await_kept(j, part)
+
+        @pl.when(t < TURNS - DEPTH)
+        def _():
+            direct_next(j, part, sent)
+
+            @pl.when(side == 0)
+            def _():
+                direct_side(j, part, sent)
+
+            start_next(t + DEPTH)
 
     def arrived_rest(j, part):
         arrived(6 - 2 * core, j, part)
@@ -194,6 +212,7 @@
         out_local(j).start()
 
     def weigh(j):
+        weights = wbuf.at[j % 2]
         for unit in range(2 * GROUP):
             block, h = unit // GROUP, unit % GROUP
             base = 2 * block
@@ -224,16 +243,16 @@
                     lax.broadcasted_iota(jnp.int32, (TILE, tok), 1)
                     > lax.broadcasted_iota(jnp.int32, (TILE, tok), 0) + r
                 )
-                wbuf[block, 0, rows_here, :] = jnp.where(ahead, first, 0.0).astype(wbuf.dtype)
-                wbuf[block, 4, rows_here, :] = jnp.where(ahead, 0.0, first).astype(wbuf.dtype)
+                weights[block, 0, rows_here, :] = jnp.where(ahead, first, 0.0).astype(wbuf.dtype)
+                weights[block, 4, rows_here, :] = jnp.where(ahead, 0.0, first).astype(wbuf.dtype)
                 for i in range(1, 4):
-                    wbuf[block, i, rows_here, :] = weight[:, i * tok:(i + 1) * tok].astype(wbuf.dtype)
+                    weights[block, i, rows_here, :] = weight[:, i * tok:(i + 1) * tok].astype(wbuf.dtype)
 
     def blend(j, block):
         base = 2 * block
         out = None
         for i in range(5):
-            term = jnp.dot(wbuf[block, i], kv[base + i, j, 1], preferred_element_type=jnp.float32)
+            term = jnp.dot(wbuf[j % 2, block, i], kv[base + i, j, 1], preferred_element_type=jnp.float32)
             out = term if out is None else out + term
         out = out.astype(obuf.dtype)
         for h in range(GROUP):
@@ -280,47 +299,54 @@
 
     pl.semaphore_wait(barrier, 3 + jnp.where(has_next, 2, 0) + jnp.where(has_prev, 2, 0))
 
-    for j, part in ((0, 0), (0, 1), (1, 0)):
+    for t, (j, part) in enumerate(((0, 0), (1, 0), (0, 1), (2, 0), (1, 1), (3, 0), (2, 1), (3, 1))):
         staged(j, part)
-        direct_next(j, part, launch)
-        direct_side(j, part, launch)
+        if t < DEPTH:
+            direct_next(j, part, launch)
+            direct_side(j, part, launch)
+        else:
+            @pl.when(side == 1)
+            def _():
+                direct_side(j, part, launch)
+
         if part == 0:
             q_swap(j, core).start()
-    for j, part in ((1, 1), (2, 0), (2, 1), (3, 0), (3, 1)):
-        staged(j, part)
-        if part == 0:
-            q_swap(j, core).start()
-
-    @pl.when(side == 1)
-    def _():
-        direct_side(1, 1, launch)
-        direct_side(2, 0, launch)
-
-    def step(j, carry):
-        @pl.when(j < HALF_KV)
-        def _():
-            exchange(j, 0)
-
-        @pl.when(j > 0)
-        def _():
-            weigh_chunk(j - 1)
-
-        @pl.when(j < HALF_KV)
-        def _():
-            exchange(j, 1)
-
-        @pl.when(j > 0)
-        def _():
-            blend_chunk(j - 1)
+
+    def step(t, carry):
+        @pl.when(t < TURNS)
+        def _():
+            exchange(t)
+
+        @pl.when(jnp.logical_or(t == 4, t >= 6))
+        def _():
+            blend_chunk(jnp.where(t == 4, 0, t - 5))
+
+        @pl.when(jnp.logical_or(t == 2, jnp.logical_and(t >= 4, t <= 6)))
+        def _():
+            weigh_chunk(jnp.where(t == 2, 0, t - 3))
 
         return carry
 
-    lax.fori_loop(0, HALF_KV + 1, step, 0)
+    lax.fori_loop(0, TURNS + 1, step, 0)
+
+    def finish_direct(t, carry):
+        j, part = turn(t)
+        forwards(j, part, lambda copy, slot: copy.wait_send())
+
+        @pl.when(t >= TURNS - DEPTH)
+        def _():
+            direct_next(j, part, sent)
+
+        @pl.when(jnp.logical_or(side == 1, t >= TURNS - DEPTH))
+        def _():
+            direct_side(j, part, sent)
+
+        return carry
+
+    lax.fori_loop(0, TURNS, finish_direct, 0)
 
     def finish(j, carry):
         q_swap(j, core).wait_send()
-        for part in (0, 1):
-            forwards(j, part, lambda copy, slot: None if copy is None else copy.wait_send())
         out_local(j).wait()
         out_remote(j, core).wait_send()
         out_remote(j, 1 - core).wait_recv()
@@ -344,7 +370,7 @@
             pltpu.VMEM((HALF_KV, 2, tok, HEAD_DIM), kind),
             pltpu.VMEM((2, HALF_KV, tok, wide), kind),
             pltpu.VMEM((2, tok, WINDOW), jnp.float32),
-            pltpu.VMEM((2, 5, GROUP * tok, tok), kind),
+            pltpu.VMEM((2, 2, 5, GROUP * tok, tok), kind),
             pltpu.VMEM((2, HALF_KV, tok, wide), kind),
             dma((HALF_KV, 4)),
             dma((HALF_KV,)),

time: 40.5 us -> 44.4 us (1.096)
  Pallas kernels: 37.9 us -> 41.7 us
    pallas_call x1, Pallas kernels: 37.9 us -> 41.7 us  [fused_body(): pl.pallas_call(functools.partial(fused_kernel, rows), out_shape=jax.Shape...]
where the time goes in v6:
time: 44.4 us; the launch traced here: 44.1 us
  Pallas kernels  41.7 us (94%)
  local copies, waits for them, and re-layouts  2.3 us (5%)
    pallas_call x1, Pallas kernels, fused_body(): pl.pallas_call(functools.partial(fused_kernel, rows), out_shape=jax.Shape...  41.7 us
    unnamed x1, local copies, waits for them, and re-layouts  2.3 us

profile of v6, /device:TPU:16, one launch (start us, length us, event | category | flops | bytes accessed | tf_op | source)
XLA Modules:
  0.0 44.1 jit_solution(7540077118196769787)
XLA Ops:
  0.0 41.7 %window_attention.1 = bf16[256,2048]{1,0:T(8,128)(2,1)} custom-call(bf16[256,2048]{1,0:T(8,128)(2,1)} %q_ref.1, bf16[256,1024]{1,0:T(8,128)(2,1)} %k_ref.1, bf16[256,1024]{1,0:T(8,128)(2,1)} %v_ref.1), custom_call_target="tpu_custom_call" | custom-call | flops 2684354560 | bytes 3145728 | tf_op jit(solution)/shard_map/window_attention/pallas_call | solution.py:363
  41.7 2.3 %copy.5 = bf16[256,2048]{1,0:T(8,128)(2,1)} copy(bf16[256,2048]{1,0:T(8,128)(2,1)} %window_attention.1) | data formatting | bytes 2097152

commit v7 on v6

--- a/solution.py
+++ b/solution.py
@@ -161,10 +161,7 @@
     def start_next(t):
         j, part = turn(t)
         direct_next(j, part, launch)
-
-        @pl.when(side == 0)
-        def _():
-            direct_side(j, part, launch)
+        direct_side(j, part, launch)
 
     def exchange(t):
         j, part = turn(t)
@@ -179,11 +176,7 @@
         @pl.when(t < TURNS - DEPTH)
         def _():
             direct_next(j, part, sent)
-
-            @pl.when(side == 0)
-            def _():
-                direct_side(j, part, sent)
-
+            direct_side(j, part, sent)
             start_next(t + DEPTH)
 
     def arrived_rest(j, part):
@@ -304,11 +297,6 @@
         if t < DEPTH:
             direct_next(j, part, launch)
             direct_side(j, part, launch)
-        else:
-            @pl.when(side == 1)
-            def _():
-                direct_side(j, part, launch)
-
         if part == 0:
             q_swap(j, core).start()
 
@@ -321,9 +309,9 @@
         def _():
             blend_chunk(jnp.where(t == 4, 0, t - 5))
 
-        @pl.when(jnp.logical_or(t == 2, jnp.logical_and(t >= 4, t <= 6)))
-        def _():
-            weigh_chunk(jnp.where(t == 2, 0, t - 3))
+        @pl.when(jnp.logical_or(jnp.logical_or(t == 2, t == 4), jnp.logical_or(t == 5, t == 7)))
+        def _():
+            weigh_chunk(jnp.where(t == 2, 0, jnp.where(t == 7, 3, t - 3)))
 
         return carry
 
@@ -336,9 +324,6 @@
         @pl.when(t >= TURNS - DEPTH)
         def _():
             direct_next(j, part, sent)
-
-        @pl.when(jnp.logical_or(side == 1, t >= TURNS - DEPTH))
-        def _():
             direct_side(j, part, sent)
 
         return carry

time: 44.4 us -> 41.8 us (0.941)
  Pallas kernels: 41.7 us -> 39.2 us
    pallas_call x1, Pallas kernels: 41.7 us -> 39.2 us  [fused_body(): pl.pallas_call(functools.partial(fused_kernel, rows), out_shape=jax.Shape...]
where the time goes in v7:
time: 41.8 us; the launch traced here: 41.5 us
  Pallas kernels  39.2 us (94%)
  local copies, waits for them, and re-layouts  2.3 us (6%)
    pallas_call x1, Pallas kernels, fused_body(): pl.pallas_call(functools.partial(fused_kernel, rows), out_shape=jax.Shape...  39.2 us
    unnamed x1, local copies, waits for them, and re-layouts  2.3 us

profile of v7, /device:TPU:16, one launch (start us, length us, event | category | flops | bytes accessed | tf_op | source)
XLA Modules:
  0.0 41.5 jit_solution(10529897620901319094)
XLA Ops:
  0.0 39.2 %window_attention.1 = bf16[256,2048]{1,0:T(8,128)(2,1)} custom-call(bf16[256,2048]{1,0:T(8,128)(2,1)} %q_ref.1, bf16[256,1024]{1,0:T(8,128)(2,1)} %k_ref.1, bf16[256,1024]{1,0:T(8,128)(2,1)} %v_ref.1), custom_call_target="tpu_custom_call" | custom-call | flops 2684354560 | bytes 3145728 | tf_op jit(solution)/shard_map/window_attention/pallas_call | solution.py:348
  39.2 2.3 %copy.5 = bf16[256,2048]{1,0:T(8,128)(2,1)} copy(bf16[256,2048]{1,0:T(8,128)(2,1)} %window_attention.1) | data formatting | bytes 2097152

commit v8 on v7

--- a/solution.py
+++ b/solution.py
@@ -161,7 +161,17 @@
     def start_next(t):
         j, part = turn(t)
         direct_next(j, part, launch)
-        direct_side(j, part, launch)
+
+        @pl.when(side == 0)
+        def _():
+            direct_side(j, part, launch)
+
+    def start_side(t):
+        j, part = turn(t)
+
+        @pl.when(jnp.logical_and(side == 1, t < TURNS))
+        def _():
+            direct_side(j, part, launch)
 
     def exchange(t):
         j, part = turn(t)
@@ -175,9 +185,17 @@
 
         @pl.when(t < TURNS - DEPTH)
         def _():
-            direct_next(j, part, sent)
-            direct_side(j, part, sent)
+            @pl.when(t > 0)
+            def _():
+                direct_next(j, part, sent)
+                direct_side(j, part, sent)
+
+            @pl.when(t == 0)
+            def _():
+                start_next(DEPTH - 1)
+
             start_next(t + DEPTH)
+            start_side(t + DEPTH + 1)
 
     def arrived_rest(j, part):
         arrived(6 - 2 * core, j, part)
@@ -294,9 +312,12 @@
 
     for t, (j, part) in enumerate(((0, 0), (1, 0), (0, 1), (2, 0), (1, 1), (3, 0), (2, 1), (3, 1))):
         staged(j, part)
-        if t < DEPTH:
+        if t < DEPTH - 1:
             direct_next(j, part, launch)
             direct_side(j, part, launch)
+        elif t < DEPTH + 1:
+            start_side(t)
+
         if part == 0:
             q_swap(j, core).start()
 
@@ -321,7 +342,7 @@
         j, part = turn(t)
         forwards(j, part, lambda copy, slot: copy.wait_send())
 
-        @pl.when(t >= TURNS - DEPTH)
+        @pl.when(jnp.logical_or(t == 0, t >= TURNS - DEPTH))
         def _():
             direct_next(j, part, sent)
             direct_side(j, part, sent)
@@ -368,14 +389,14 @@
             dma((HALF_KV,)),
         ],
         compiler_params=pltpu.CompilerParams(
-            collective_id=0, has_side_effects=True, vmem_limit_bytes=58 * 1024 * 1024
+            collective_id=0, has_side_effects=True, vmem_limit_bytes=40 * 1024 * 1024
         ),
         cost_estimate=pl.CostEstimate(
             flops=4 * tok * HEADS * HEAD_DIM * (WINDOW + tok), bytes_accessed=6 * tok * HEADS * HEAD_DIM,
             transcendentals=tok * HEADS * WINDOW,
         ),
         name="window_attention",
-    )(queries, keys, values)
+    )(*(pltpu.with_memory_space_constraint(x, pltpu.HBM) for x in (queries, keys, values)))
 
 
 def from_behind(x, axis, by):

time: 41.8 us -> 40.3 us (0.964)
  local copies, waits for them, and re-layouts: 2.3 us -> 0.97 us
    unnamed x1, local copies, waits for them, and re-layouts: 2.3 us -> 0.97 us
where the time goes in v8:
time: 40.3 us; the launch traced here: 39.9 us
  Pallas kernels  38.9 us (97%)
  local copies, waits for them, and re-layouts  0.97 us (2%)
    pallas_call x1, Pallas kernels, fused_body(): pl.pallas_call(functools.partial(fused_kernel, rows), out_shape=jax.Shape...  38.9 us
    unnamed x1, local copies, waits for them, and re-layouts  0.97 us

profile of v8, /device:TPU:16, one launch (start us, length us, event | category | flops | bytes accessed | tf_op | source)
XLA Modules:
  0.0 39.9 jit_solution(8733424747145595128)
XLA Ops:
  0.0 38.9 %window_attention.1 = bf16[256,2048]{1,0:T(8,128)(2,1)S(1)} custom-call(bf16[256,2048]{1,0:T(8,128)(2,1)} %q_ref.1, bf16[256,1024]{1,0:T(8,128)(2,1)} %k_ref.1, bf16[256,1024]{1,0:T(8,128)(2,1)} %v_ref.1), custom_call_target="tpu_custom_call" | custom-call | flops 2684354560 | bytes 3145728 | tf_op jit(solution)/shard_map/window_attention/pallas_call | solution.py:369
  38.9 1.0 %copy.5 = bf16[256,2048]{1,0:T(8,128)(2,1)} copy(bf16[256,2048]{1,0:T(8,128)(2,1)S(1)} %window_attention.1) | data formatting | bytes 2097152

commit v9 on v5

--- a/solution.py
+++ b/solution.py
@@ -357,14 +357,14 @@
             dma((HALF_KV,)),
         ],
         compiler_params=pltpu.CompilerParams(
-            collective_id=0, has_side_effects=True, vmem_limit_bytes=58 * 1024 * 1024
+            collective_id=0, has_side_effects=True, vmem_limit_bytes=40 * 1024 * 1024
         ),
         cost_estimate=pl.CostEstimate(
             flops=4 * tok * HEADS * HEAD_DIM * (WINDOW + tok), bytes_accessed=6 * tok * HEADS * HEAD_DIM,
             transcendentals=tok * HEADS * WINDOW,
         ),
         name="window_attention",
-    )(queries, keys, values)
+    )(*(pltpu.with_memory_space_constraint(x, pltpu.HBM) for x in (queries, keys, values)))
 
 
 def from_behind(x, axis, by):

time: 40.5 us -> 39 us (0.963)
  local copies, waits for them, and re-layouts: 2.3 us -> 0.97 us
  Pallas kernels: 37.9 us -> 37.4 us
    unnamed x1, local copies, waits for them, and re-layouts: 2.3 us -> 0.97 us
    pallas_call x1, Pallas kernels: 37.9 us -> 37.4 us  [fused_body(): pl.pallas_call(functools.partial(fused_kernel, rows), out_shape=jax.Shape...]
where the time goes in v9:
time: 39 us; the launch traced here: 38.3 us
  Pallas kernels  37.4 us (96%)
  local copies, waits for them, and re-layouts  0.97 us (2%)
    pallas_call x1, Pallas kernels, fused_body(): pl.pallas_call(functools.partial(fused_kernel, rows), out_shape=jax.Shape...  37.4 us
    unnamed x1, local copies, waits for them, and re-layouts  0.97 us

profile of v9, /device:TPU:16, one launch (start us, length us, event | category | flops | bytes accessed | tf_op | source)
XLA Modules:
  0.0 38.3 jit_solution(9909895534820453056)
XLA Ops:
  0.0 37.4 %window_attention.1 = bf16[256,2048]{1,0:T(8,128)(2,1)S(1)} custom-call(bf16[256,2048]{1,0:T(8,128)(2,1)} %q_ref.1, bf16[256,1024]{1,0:T(8,128)(2,1)} %k_ref.1, bf16[256,1024]{1,0:T(8,128)(2,1)} %v_ref.1), custom_call_target="tpu_custom_call" | custom-call | flops 2684354560 | bytes 3145728 | tf_op jit(solution)/shard_map/window_attention/pallas_call | solution.py:337
  37.4 1.0 %copy.5 = bf16[256,2048]{1,0:T(8,128)(2,1)} copy(bf16[256,2048]{1,0:T(8,128)(2,1)S(1)} %window_attention.1) | data formatting | bytes 2097152
